TPU v7x, 32 devices: a whole 2x2x4 slice. The times are simulated.
32 devices in a mesh: groups: 2 (over y), tile: 16 (over z, x, core).
Axes of the slice: x: 2, y: 2, z: 4, core: 2. Of those that a mesh axis runs over, the one named last changes fastest.
Arguments:
- object_slices: float32 [4096, 2, 2, 256], P(('groups', 'tile')), parts along dimension 0, may hold values from -4 to 4
- probe_field: float32 [256, 2, 2, 128], P(('groups', 'tile')), parts along dimension 0, may hold values from -2.5 to 2.5
- patterns: float32 [512, 128, 128], P(('groups', 'tile')), parts along dimension 0, may hold values from 0 to 2
- row_offsets: int32 [512], P(('groups', 'tile')), parts along dimension 0, may hold values from 0 to 127
- col_offsets: int32 [512], P(('groups', 'tile')), parts along dimension 0, may hold values from 0 to 128
- counts: int32 [32], P(('groups', 'tile')), parts along dimension 0, may hold values from 1 to 16, as said below
Outputs:
- object_grad: float32 [4096, 2, 2, 256], P(('groups', 'tile')), parts along dimension 0
- probe_grad: float32 [256, 2, 2, 128], P(('groups', 'tile')), parts along dimension 0
There are 2 independent parts, one for each index of `groups`. A program takes and returns all parts, laid end to end along the dimension named above; each array names one. Nothing has to cross between parts.
Inputs may be any that keep to these rules, and one draw needn't show every extreme that they name: `counts`: each tile has 1 to 16 live slots, and one tile of every draw has 16.
All inputs are finite; a program needn't handle non-finite values.
Results may differ from a plain program's by a relative error of at most 0.0003.
Values sent between devices are 32-bit elements; how exact they have to be, the bound alone decides.
No kernel may reach another device: no remote copies, remote signals or barrier semaphores. Data moves between devices by JAX's collectives and lax.ppermute only.
A program may use at most 64 MiB of HBM per device.

v0:
```python
import math

import jax
import jax.numpy as jnp
from jax import lax
from jax.sharding import PartitionSpec as P

GROUP_DEV = 16


KAPPA = 4.0
HIGHEST = lax.Precision.HIGHEST


def shifted(block, axis, distance):
    devices = range(lax.axis_size(axis))
    route = [((i - distance) % len(devices), i) for i in devices]
    return lax.ppermute(block, axis, route)


def partner_2(value, axis, bit):
    return lax.ppermute(value, axis, [(i, i ^ 1 << bit) for i in range(lax.axis_size(axis))])


def tables(extent):
    counter = jnp.arange(extent, dtype=jnp.int32)
    product = counter[:, None] * counter[None, :] % extent
    angle = product.astype(jnp.float32) * (-2.0 * math.pi / extent)
    norm_factor = 1.0 / math.sqrt(extent)
    freq_axis = ((counter + extent // 2) % extent - extent // 2).astype(jnp.float32) / extent
    phase = -math.pi * KAPPA * (freq_axis[:, None] ** 2 + freq_axis[None, :] ** 2)
    return (
        jnp.cos(angle) * norm_factor,
        jnp.sin(angle) * norm_factor,
        jnp.cos(phase),
        jnp.sin(phase),
    )


def multiply(left_side, right_side):
    return jnp.dot(left_side, right_side, precision=HIGHEST, preferred_element_type=jnp.float32)


def transform(real_part, imag_part, dft_real, dft_imag):
    extent = real_part.shape[0]
    mode_count = real_part.shape[1]
    flat_real = real_part.reshape(extent, mode_count * extent)
    flat_imag = imag_part.reshape(extent, mode_count * extent)
    rows_real = multiply(dft_real, flat_real) - multiply(dft_imag, flat_imag)
    rows_imag = multiply(dft_real, flat_imag) + multiply(dft_imag, flat_real)
    rows_real = rows_real.reshape(extent * mode_count, extent)
    rows_imag = rows_imag.reshape(extent * mode_count, extent)
    cols_real = multiply(rows_real, dft_real) - multiply(rows_imag, dft_imag)
    cols_imag = multiply(rows_real, dft_imag) + multiply(rows_imag, dft_real)
    return (
        cols_real.reshape(extent, mode_count, extent),
        cols_imag.reshape(extent, mode_count, extent),
    )


def carry_over(real_part, imag_part, table, factor):
    dft_real, dft_imag, kern_real, kern_imag = table
    freq_real, freq_imag = transform(real_part, imag_part, dft_real, dft_imag)
    turned_real = freq_real * kern_real[:, None, :] - factor * freq_imag * kern_imag[:, None, :]
    turned_imag = freq_imag * kern_real[:, None, :] + factor * freq_real * kern_imag[:, None, :]
    return transform(turned_real, turned_imag, dft_real, -dft_imag)


def position_terms(window, measured, probe_real, probe_imag, table):
    layers = window.shape[1]
    dft_real, dft_imag = (table[0], table[1])
    obj_real = [window[:, layer_no, 0, :][:, None, :] for layer_no in range(layers)]
    obj_imag = [window[:, layer_no, 1, :][:, None, :] for layer_no in range(layers)]
    entering = [(probe_real, probe_imag)]
    leave_real, leave_imag = (probe_real, probe_imag)
    for layer_no in range(layers):
        enter_real, enter_imag = entering[layer_no]
        leave_real = enter_real * obj_real[layer_no] - enter_imag * obj_imag[layer_no]
        leave_imag = enter_real * obj_imag[layer_no] + enter_imag * obj_real[layer_no]
        if layer_no + 1 < layers:
            entering.append(carry_over(leave_real, leave_imag, table, 1.0))
    far_real, far_imag = transform(leave_real, leave_imag, dft_real, dft_imag)
    intensity = jnp.sum(far_real * far_real + far_imag * far_imag, axis=1)
    weighting = (2.0 * (intensity - measured))[:, None, :]
    back_real, back_imag = transform(
        weighting * far_real, weighting * far_imag, dft_real, -dft_imag
    )
    layer_grads = [None] * layers
    in_real, in_imag = (back_real, back_imag)
    for layer_no in reversed(range(layers)):
        enter_real, enter_imag = entering[layer_no]
        grad_real = jnp.sum(enter_real * back_real + enter_imag * back_imag, axis=1)
        grad_imag = jnp.sum(enter_real * back_imag - enter_imag * back_real, axis=1)
        layer_grads[layer_no] = jnp.stack([grad_real, grad_imag], axis=1)
        in_real = obj_real[layer_no] * back_real + obj_imag[layer_no] * back_imag
        in_imag = obj_real[layer_no] * back_imag - obj_imag[layer_no] * back_real
        if layer_no > 0:
            back_real, back_imag = carry_over(in_real, in_imag, table, -1.0)
    return (jnp.stack(layer_grads, axis=1), in_real, in_imag)


def shards(object_slices, probe_field, patterns, row_offsets, col_offsets, counts):
    tile_rows = object_slices.shape[0]
    layers = object_slices.shape[1]
    extent = probe_field.shape[3]
    upper_rows = shifted(object_slices, "tile", -1)
    extended = jnp.concatenate([object_slices, upper_rows], axis=0)
    my_index = lax.axis_index("tile")
    levels = GROUP_DEV.bit_length() - 1
    assembled = probe_field
    for bit_no in range(levels):
        partner = partner_2(assembled, "tile", bit_no)
        upper_half = my_index >> bit_no & 1 == 1
        assembled = jnp.where(
            upper_half,
            jnp.concatenate([partner, assembled], axis=0),
            jnp.concatenate([assembled, partner], axis=0),
        )
    probe_real = assembled[:, :, 0, :]
    probe_imag = assembled[:, :, 1, :]
    table = tables(extent)
    anchor = jnp.zeros((), jnp.int32)

    def cut_window(row_start, col_start):
        return lax.dynamic_slice(
            extended, (row_start, anchor, anchor, col_start), (extent, layers, 2, extent)
        )

    def deposit(accumulated, patch_grad, row_start, col_start):
        corner = (row_start, anchor, anchor, col_start)
        current = lax.dynamic_slice(accumulated, corner, (extent, layers, 2, extent))
        return lax.dynamic_update_slice(accumulated, current + patch_grad, corner)

    def own_step(position, carry):
        accumulated, grad_real, grad_imag = carry
        row_start = row_offsets[position]
        col_start = col_offsets[position]
        patch_grad, term_real, term_imag = position_terms(
            cut_window(row_start, col_start), patterns[position], probe_real, probe_imag, table
        )
        return (
            deposit(accumulated, patch_grad, row_start, col_start),
            grad_real + term_real,
            grad_imag + term_imag,
        )

    starting = (
        jnp.zeros(extended.shape, jnp.float32),
        jnp.zeros(probe_real.shape, jnp.float32),
        jnp.zeros(probe_real.shape, jnp.float32),
    )
    own_count = counts[0]
    accumulated, grad_real, grad_imag = lax.fori_loop(0, own_count, own_step, starting)
    back_rows = shifted(accumulated[tile_rows:], "tile", 1)
    object_grad = accumulated[:tile_rows].at[:extent].add(back_rows)
    combined = jnp.stack([grad_real, grad_imag], axis=2)
    share = extent // GROUP_DEV
    for bit_no in range(levels):
        combined = combined + partner_2(combined, "tile", bit_no)
    member = my_index % GROUP_DEV
    probe_grad = lax.dynamic_slice_in_dim(combined, member * share, share, 0)
    return (object_grad, probe_grad)


def solution(mesh):
    in_specs = (
        P(("groups", "tile"), None, None, None),
        P(("groups", "tile"), None, None, None),
        P(("groups", "tile"), None, None),
        P(("groups", "tile")),
        P(("groups", "tile")),
        P(("groups", "tile")),
    )
    out_specs = (P(("groups", "tile"), None, None, None), P(("groups", "tile"), None, None, None))
    return jax.shard_map(shards, mesh=mesh, in_specs=in_specs, out_specs=out_specs, check_vma=False)
```

profile of v0, /device:TPU:0, one launch (start us, length us, event | category | flops | bytes accessed | tf_op | source)
XLA Modules:
  0.0 1279.8 jit_solution(15414534998229008711)
XLA Ops:
  0.6 0.7 copy.27
  1.9 0.8 collective-permute-done.1
  2.7 2.9 collective-permute-start.2
  5.6 1.9 collective-permute-done.2
  7.6 2.2 collective-permute-start.3
  9.7 1.1 copy.26
  10.9 1.8 collective-permute-start
  12.8 2.4 collective-permute-start.4
  15.2 11.0 collective-permute-done.4
  26.4 1.1 pad_maximum_fusion
  27.9 0.6 copy-done.2
  28.6 641.9 %while.20 = (s32[]{:T(128)}, f32[256,2,2,256]{3,2,1,0:T(2,128)S(1)}, f32[128,2,128]{2,1,0:T(2,128)S(1)}, f32[128,2,128]{2,1,0:T(2,128)S(1)}, s32[]{:T(128)}, /*i...) while((s32[]{:T(128)}, ...), condition=%wide.region_6.7_spmd.clone.clone.clone, body=%wide.region_0.6_spmd.clone.clone.clone.sunk | while | flops 2430926848 | bytes 44106640 | solution.py:153
  29.2 0.7 dynamic_slice.52
  31.9 0.6 dynamic_slice.51
  49.3 0.9 fusion.544
  65.8 42.8 %dynamic_update_slice.8 = f32[256,2,2,256]{3,2,1,0:T(2,128)S(1)} dynamic-update-slice(f32[256,2,2,256]{3,2,1,0:T(2,128)S(1)} %get-tuple-element.692, f32[128,2,2,128]{3,2,1,0:T(2,128)S(1)} %maximum_add_fusion.2, s32[]{:T(128)S(6)} %select_n.404, s32[]{:T(128)} %constant.106.clone.1..sunk, s32[]{:T(128)} %constant.106.clone.1..sunk, s32[]{:T(128)S(6)} %select_n.405) | dynamic-update-slice | bytes 524292 | tf_op jit(solution)/shard_map/while/body/dynamic_update_slice | solution.py:132
  109.4 0.7 dynamic_slice.52
  112.0 0.6 dynamic_slice.51
  129.5 0.9 fusion.544
  146.0 42.8 %dynamic_update_slice.8 = f32[256,2,2,256]{3,2,1,0:T(2,128)S(1)} dynamic-update-slice(f32[256,2,2,256]{3,2,1,0:T(2,128)S(1)} %get-tuple-element.692, f32[128,2,2,128]{3,2,1,0:T(2,128)S(1)} %maximum_add_fusion.2, s32[]{:T(128)S(6)} %select_n.404, s32[]{:T(128)} %constant.106.clone.1..sunk, s32[]{:T(128)} %constant.106.clone.1..sunk, s32[]{:T(128)S(6)} %select_n.405) | dynamic-update-slice | bytes 524292 | tf_op jit(solution)/shard_map/while/body/dynamic_update_slice | solution.py:132
  189.5 0.7 dynamic_slice.52
  192.2 0.6 dynamic_slice.51
  209.6 0.9 fusion.544
  226.2 42.8 %dynamic_update_slice.8 = f32[256,2,2,256]{3,2,1,0:T(2,128)S(1)} dynamic-update-slice(f32[256,2,2,256]{3,2,1,0:T(2,128)S(1)} %get-tuple-element.692, f32[128,2,2,128]{3,2,1,0:T(2,128)S(1)} %maximum_add_fusion.2, s32[]{:T(128)S(6)} %select_n.404, s32[]{:T(128)} %constant.106.clone.1..sunk, s32[]{:T(128)} %constant.106.clone.1..sunk, s32[]{:T(128)S(6)} %select_n.405) | dynamic-update-slice | bytes 524292 | tf_op jit(solution)/shard_map/while/body/dynamic_update_slice | solution.py:132
  269.7 0.7 dynamic_slice.52
  272.3 0.6 dynamic_slice.51
  289.8 0.9 fusion.544
  306.3 42.8 %dynamic_update_slice.8 = f32[256,2,2,256]{3,2,1,0:T(2,128)S(1)} dynamic-update-slice(f32[256,2,2,256]{3,2,1,0:T(2,128)S(1)} %get-tuple-element.692, f32[128,2,2,128]{3,2,1,0:T(2,128)S(1)} %maximum_add_fusion.2, s32[]{:T(128)S(6)} %select_n.404, s32[]{:T(128)} %constant.106.clone.1..sunk, s32[]{:T(128)} %constant.106.clone.1..sunk, s32[]{:T(128)S(6)} %select_n.405) | dynamic-update-slice | bytes 524292 | tf_op jit(solution)/shard_map/while/body/dynamic_update_slice | solution.py:132
  349.9 0.7 dynamic_slice.52
  352.5 0.6 dynamic_slice.51
  369.9 0.9 fusion.544
  386.5 42.8 %dynamic_update_slice.8 = f32[256,2,2,256]{3,2,1,0:T(2,128)S(1)} dynamic-update-slice(f32[256,2,2,256]{3,2,1,0:T(2,128)S(1)} %get-tuple-element.692, f32[128,2,2,128]{3,2,1,0:T(2,128)S(1)} %maximum_add_fusion.2, s32[]{:T(128)S(6)} %select_n.404, s32[]{:T(128)} %constant.106.clone.1..sunk, s32[]{:T(128)} %constant.106.clone.1..sunk, s32[]{:T(128)S(6)} %select_n.405) | dynamic-update-slice | bytes 524292 | tf_op jit(solution)/shard_map/while/body/dynamic_update_slice | solution.py:132
  430.0 0.7 dynamic_slice.52
  450.1 0.9 fusion.544
  466.6 42.8 %dynamic_update_slice.8 = f32[256,2,2,256]{3,2,1,0:T(2,128)S(1)} dynamic-update-slice(f32[256,2,2,256]{3,2,1,0:T(2,128)S(1)} %get-tuple-element.692, f32[128,2,2,128]{3,2,1,0:T(2,128)S(1)} %maximum_add_fusion.2, s32[]{:T(128)S(6)} %select_n.404, s32[]{:T(128)} %constant.106.clone.1..sunk, s32[]{:T(128)} %constant.106.clone.1..sunk, s32[]{:T(128)S(6)} %select_n.405) | dynamic-update-slice | bytes 524292 | tf_op jit(solution)/shard_map/while/body/dynamic_update_slice | solution.py:132
  510.2 0.7 dynamic_slice.52
  530.3 0.9 fusion.544
  546.8 42.8 %dynamic_update_slice.8 = f32[256,2,2,256]{3,2,1,0:T(2,128)S(1)} dynamic-update-slice(f32[256,2,2,256]{3,2,1,0:T(2,128)S(1)} %get-tuple-element.692, f32[128,2,2,128]{3,2,1,0:T(2,128)S(1)} %maximum_add_fusion.2, s32[]{:T(128)S(6)} %select_n.404, s32[]{:T(128)} %constant.106.clone.1..sunk, s32[]{:T(128)} %constant.106.clone.1..sunk, s32[]{:T(128)S(6)} %select_n.405) | dynamic-update-slice | bytes 524292 | tf_op jit(solution)/shard_map/while/body/dynamic_update_slice | solution.py:132
  590.3 0.7 dynamic_slice.52
  610.4 0.9 fusion.544
  627.0 42.8 %dynamic_update_slice.8 = f32[256,2,2,256]{3,2,1,0:T(2,128)S(1)} dynamic-update-slice(f32[256,2,2,256]{3,2,1,0:T(2,128)S(1)} %get-tuple-element.692, f32[128,2,2,128]{3,2,1,0:T(2,128)S(1)} %maximum_add_fusion.2, s32[]{:T(128)S(6)} %select_n.404, s32[]{:T(128)} %constant.106.clone.1..sunk, s32[]{:T(128)} %constant.106.clone.1..sunk, s32[]{:T(128)S(6)} %select_n.405) | dynamic-update-slice | bytes 524292 | tf_op jit(solution)/shard_map/while/body/dynamic_update_slice | solution.py:132
  670.8 1.5 collective-permute-done.6
  673.0 8.0 collective-permute-done.7
  681.5 7.5 collective-permute-done.8
  689.1 579.3 %collective-permute-start.9 = (f32[128,2,2,128]{3,2,1,0:T(2,128)S(1)}, f32[128,2,2,128]{3,2,1,0:T(2,128)S(1)}, u32[]{:S(2)}, u32[]{:S(2)}) collective-permute-start(f32[128,2,2,128]{3,2,1,0:T(2,128)S(1)} %add.404), channel_id=1, source_target_pairs={{0,8},{1,9},{2,10},{3,11},{4,12},{5,13},{6,14},{7,15},{8,0},{9,1},... | collective-permute-start | bytes 786440 | tf_op jit(solution)/shard_map/ppermute | solution.py:22
  1268.4 1.1 slice_add_fusion
  1269.4 9.7 collective-permute-done.9
  1279.1 0.6 dynamic-slice_add_fusion
  (868 shorter events, 243.4 us)
Async XLA Ops:
  1.4 1.4 collective-permute-start.1
  2.7 4.8 collective-permute-start.2
  7.6 5.1 collective-permute-start.3
  10.9 15.5 %collective-permute-start = (f32[128,2,2,256]{3,0,2,1:T(8,128)S(1)}, f32[128,2,2,256]{3,0,2,1:T(8,128)}, u32[]{:S(2)}, u32[]{:S(2)}) collective-permute-start(f32[128,2,2,256]{3,0,2,1:T(8,128)S(1)} %copy.26), channel_id=1, source_target_pairs={{1,0},{2,1},{3,2},{4,3},{5,4},{6,5},{7,6},{8,7},{9,8},{10,9},{11,1... | collective-permute-start | bytes 1572872 | tf_op jit(solution)/shard_map/ppermute | solution.py:18
  12.8 13.4 %collective-permute-start.4 = (f32[64,2,2,128]{3,1,0,2:T(2,128)S(1)}, f32[64,2,2,128]{3,1,0,2:T(2,128)S(1)}, u32[]{:S(2)}, u32[]{:S(2)}) collective-permute-start(f32[64,2,2,128]{3,1,0,2:T(2,128)S(1)} %maximum_select_fusion.1), channel_id=1, source_target_pairs={{0,8},{1,9},{2,10},{3,11},{4,12},{5,13},{6,14},{7,15},{8,0},{9,1},... | collective-permute-start | bytes 393224 | tf_op jit(solution)/shard_map/ppermute | solution.py:22
  27.9 0.7 copy-start.2
  27.9 0.7 copy-start.3
  29.2 5.3 copy-start
  65.1 43.6 %copy-start.1 = (f32[256,2,2,256]{3,0,2,1:T(8,128)S(1)}, f32[256,2,2,256]{3,0,2,1:T(8,128)}, u32[]{:S(2)}) copy-start(f32[256,2,2,256]{3,0,2,1:T(8,128)} %copy-done) | copy-start | bytes 3145732 | tf_op jit(solution)/shard_map/while
  109.4 5.3 copy-start
  145.2 43.6 %copy-start.1 = (f32[256,2,2,256]{3,0,2,1:T(8,128)S(1)}, f32[256,2,2,256]{3,0,2,1:T(8,128)}, u32[]{:S(2)}) copy-start(f32[256,2,2,256]{3,0,2,1:T(8,128)} %copy-done) | copy-start | bytes 3145732 | tf_op jit(solution)/shard_map/while
  189.5 5.3 copy-start
  225.4 43.6 %copy-start.1 = (f32[256,2,2,256]{3,0,2,1:T(8,128)S(1)}, f32[256,2,2,256]{3,0,2,1:T(8,128)}, u32[]{:S(2)}) copy-start(f32[256,2,2,256]{3,0,2,1:T(8,128)} %copy-done) | copy-start | bytes 3145732 | tf_op jit(solution)/shard_map/while
  269.7 5.3 copy-start
  305.6 43.6 %copy-start.1 = (f32[256,2,2,256]{3,0,2,1:T(8,128)S(1)}, f32[256,2,2,256]{3,0,2,1:T(8,128)}, u32[]{:S(2)}) copy-start(f32[256,2,2,256]{3,0,2,1:T(8,128)} %copy-done) | copy-start | bytes 3145732 | tf_op jit(solution)/shard_map/while
  349.9 5.3 copy-start
  385.7 43.6 %copy-start.1 = (f32[256,2,2,256]{3,0,2,1:T(8,128)S(1)}, f32[256,2,2,256]{3,0,2,1:T(8,128)}, u32[]{:S(2)}) copy-start(f32[256,2,2,256]{3,0,2,1:T(8,128)} %copy-done) | copy-start | bytes 3145732 | tf_op jit(solution)/shard_map/while
  430.0 5.3 copy-start
  465.9 43.6 %copy-start.1 = (f32[256,2,2,256]{3,0,2,1:T(8,128)S(1)}, f32[256,2,2,256]{3,0,2,1:T(8,128)}, u32[]{:S(2)}) copy-start(f32[256,2,2,256]{3,0,2,1:T(8,128)} %copy-done) | copy-start | bytes 3145732 | tf_op jit(solution)/shard_map/while
  510.2 5.3 copy-start
  546.0 43.6 %copy-start.1 = (f32[256,2,2,256]{3,0,2,1:T(8,128)S(1)}, f32[256,2,2,256]{3,0,2,1:T(8,128)}, u32[]{:S(2)}) copy-start(f32[256,2,2,256]{3,0,2,1:T(8,128)} %copy-done) | copy-start | bytes 3145732 | tf_op jit(solution)/shard_map/while
  590.3 5.3 copy-start
  626.2 43.6 %copy-start.1 = (f32[256,2,2,256]{3,0,2,1:T(8,128)S(1)}, f32[256,2,2,256]{3,0,2,1:T(8,128)}, u32[]{:S(2)}) copy-start(f32[256,2,2,256]{3,0,2,1:T(8,128)} %copy-done) | copy-start | bytes 3145732 | tf_op jit(solution)/shard_map/while
  670.7 1.6 collective-permute-start.6
  672.6 8.4 collective-permute-start.7
  672.9 595.5 %collective-permute-start.5 = (f32[128,2,2,256]{3,2,1,0:T(2,128)S(1)}, f32[128,2,2,256]{3,2,1,0:T(2,128)S(1)}, u32[]{:S(2)}, u32[]{:S(2)}) collective-permute-start(f32[128,2,2,256]{3,2,1,0:T(2,128)S(1)} %slice.55), channel_id=1, source_target_pairs={{15,0},{0,1},{1,2},{2,3},{3,4},{4,5},{5,6},{6,7},{7,8},{8,9},{9,10... | collective-permute-start | bytes 1572872 | tf_op jit(solution)/shard_map/ppermute | solution.py:18
  681.4 7.6 collective-permute-start.8
  689.1 590.0 %collective-permute-start.9 = (f32[128,2,2,128]{3,2,1,0:T(2,128)S(1)}, f32[128,2,2,128]{3,2,1,0:T(2,128)S(1)}, u32[]{:S(2)}, u32[]{:S(2)}) collective-permute-start(f32[128,2,2,128]{3,2,1,0:T(2,128)S(1)} %add.404), channel_id=1, source_target_pairs={{0,8},{1,9},{2,10},{3,11},{4,12},{5,13},{6,14},{7,15},{8,0},{9,1},... | collective-permute-start | bytes 786440 | tf_op jit(solution)/shard_map/ppermute | solution.py:22
where the time goes:
time: 1300 us; the launch traced here: 1280 us
  starting transfers between devices  589 us (45%)
  local copies, waits for them, and re-layouts  373 us (29%)
  matrix products  204 us (16%)
  loops' own time  43.4 us (3%)
  waiting for transfers between devices  40.5 us (3%)
  other arithmetic  29 us (2%)
    ppermute x8, starting transfers between devices, partner_2(): lax.ppermute(value, axis, [(i, i ^ 1 << bit) for i in range(lax.axis_size...  587 us
    dynamic_update_slice x8, local copies, waits for them, and re-layouts, deposit(): return lax.dynamic_update_slice(accumulated, current + patch_grad, corner)  343 us
    dot_general x384, matrix products, multiply(): jnp.dot(left_side, right_side, precision=HIGHEST, preferred_element_type=...  204 us
    another operation x1, loops' own time, shards(): lax.fori_loop(0, own_count, own_step, starting)  43.4 us
    ppermute x8, waiting for transfers between devices, partner_2(): lax.ppermute(value, axis, [(i, i ^ 1 << bit) for i in range(lax.axis_size...  40.5 us
  transfers between devices with their start and end apart: 10, of which 7 were waited for; matrix products, arithmetic and copies ran while one was open for 0% of the time, Pallas kernels for 0%

commit v1 on v0

v1 whole, which is shorter than its diff:
```python
import math

import jax
import jax.numpy as jnp
import numpy as np
from jax import lax
from jax.experimental import pallas as pl
from jax.experimental.pallas import tpu as pltpu
from jax.sharding import PartitionSpec as P

GROUP_DEV = 16
KAPPA = 4.0
MODES = 2
SLICES = 2


def block_matrices(extent):
    counter = np.arange(extent)
    dft = np.exp(-2j * np.pi * (counter[:, None] * counter[None, :] % extent) / extent) / math.sqrt(extent)
    freq = ((counter + extent // 2) % extent - extent // 2) / extent
    prop = np.conj(dft) @ (np.exp(-1j * np.pi * KAPPA * freq**2)[:, None] * dft)
    stacked = []
    for matrix in (dft, prop):
        for imag_sign in (1.0, -1.0):
            re, im = matrix.real, imag_sign * matrix.imag
            full = np.block([[re, im], [-im, re]]).astype(np.float32)
            high = full.astype(jnp.bfloat16)
            low = (full - high.astype(np.float32)).astype(jnp.bfloat16)
            stacked += [high, low]
    return np.stack(stacked)


def kernel(rows_ref, cols_ref, counts_ref, own_ref, next_ref, probe_ref, patterns_ref, mats_ref,
           own_out, next_out, probe_out, obj, acc, probe, probe_acc):
    extent = patterns_ref.shape[1]
    tile_rows = own_ref.shape[0] // 8
    halves = 2

    for layer in range(SLICES):
        for half in range(halves):
            for part in range(2):
                source = (layer * halves + half) * 2 + part
                plane = (layer * 2 + part) * halves + half
                obj[plane, :tile_rows] = own_ref[pl.ds(source, tile_rows, stride=8), :]
                obj[plane, tile_rows:] = next_ref[pl.ds(source, extent, stride=8), :]
    for k in range(2 * MODES):
        probe[k] = probe_ref[pl.ds(k, extent, stride=2 * MODES), :]
    acc[...] = jnp.zeros(acc.shape, jnp.float32)
    probe_acc[...] = jnp.zeros(probe_acc.shape, jnp.float32)

    def split(value):
        high = value.astype(jnp.bfloat16)
        low = (value - high.astype(jnp.float32)).astype(jnp.bfloat16)
        return high, low

    def right(fields, kind, conj):
        high_m, low_m = mats_ref[4 * kind + 2 * conj], mats_ref[4 * kind + 2 * conj + 1]
        rows = jnp.concatenate(
            [jnp.concatenate([f[m][0], f[m][1]], axis=1) for f in fields for m in range(MODES)], axis=0)
        high, low = split(rows)
        out = jnp.dot(jnp.concatenate([high, low, high], axis=1), jnp.concatenate([high_m, high_m, low_m], axis=0),
                      preferred_element_type=jnp.float32)
        return [[[out[(i * MODES + m) * extent:(i * MODES + m + 1) * extent, c * extent:(c + 1) * extent]
                  for c in range(2)] for m in range(MODES)] for i in range(len(fields))]

    def left(fields, kind, conj):
        high_m, low_m = mats_ref[4 * kind + 2 * (1 - conj)], mats_ref[4 * kind + 2 * (1 - conj) + 1]
        cols = jnp.concatenate(
            [jnp.concatenate([f[m][0], f[m][1]], axis=0) for f in fields for m in range(MODES)], axis=1)
        high, low = split(cols)
        out = jnp.dot(jnp.concatenate([high_m, high_m, low_m], axis=1), jnp.concatenate([high, low, high], axis=0),
                      preferred_element_type=jnp.float32)
        return [[[out[c * extent:(c + 1) * extent, (i * MODES + m) * extent:(i * MODES + m + 1) * extent]
                  for c in range(2)] for m in range(MODES)] for i in range(len(fields))]

    def both(fields, kind, conj):
        return left(right(fields, kind, conj), kind, conj)

    def times(a, b):
        return [a[0] * b[0] - a[1] * b[1], a[0] * b[1] + a[1] * b[0]]

    def conj_times(a, b):
        return [a[0] * b[0] + a[1] * b[1], a[0] * b[1] - a[1] * b[0]]

    def add(a, b):
        return [a[0] + b[0], a[1] + b[1]]

    lane = lax.broadcasted_iota(jnp.int32, (extent, extent), 1)

    def run(slots):
        corners = [(rows_ref[s], cols_ref[s]) for s in slots]
        objects = []
        for r, c in corners:
            shift = lax.rem(extent - c, extent)
            layers = []
            for layer in range(SLICES):
                parts = []
                for part in range(2):
                    plane = (layer * 2 + part) * halves
                    joined = jnp.where(lane >= c, obj[plane, pl.ds(r, extent), :], obj[plane + 1, pl.ds(r, extent), :])
                    parts.append(pltpu.roll(joined, shift, 1))
                layers.append(parts)
            objects.append(layers)
        fields = [[[probe[2 * m], probe[2 * m + 1]] for m in range(MODES)] for _ in slots]
        n = range(len(slots))
        leaving = [[times(fields[i][m], objects[i][0]) for m in range(MODES)] for i in n]
        entering = both(leaving, 1, 0)
        leaving = [[times(entering[i][m], objects[i][1]) for m in range(MODES)] for i in n]
        far = both(leaving, 0, 0)
        weighted = []
        for i in n:
            intensity = far[i][0][0] ** 2 + far[i][0][1] ** 2
            for m in range(1, MODES):
                intensity += far[i][m][0] ** 2 + far[i][m][1] ** 2
            weight = 2.0 * (intensity - patterns_ref[slots[i]])
            weighted.append([[weight * far[i][m][0], weight * far[i][m][1]] for m in range(MODES)])
        back = both(weighted, 0, 1)
        grads = [[None] * SLICES for _ in n]
        for i in n:
            g = conj_times(entering[i][0], back[i][0])
            for m in range(1, MODES):
                g = add(g, conj_times(entering[i][m], back[i][m]))
            grads[i][1] = g
        incoming = [[conj_times(objects[i][1], back[i][m]) for m in range(MODES)] for i in n]
        back = both(incoming, 1, 1)
        for i in n:
            g = conj_times(fields[i][0], back[i][0])
            for m in range(1, MODES):
                g = add(g, conj_times(fields[i][m], back[i][m]))
            grads[i][0] = g
            for m in range(MODES):
                q = conj_times(objects[i][0], back[i][m])
                probe_acc[2 * m] += q[0]
                probe_acc[2 * m + 1] += q[1]
        for i, (r, c) in enumerate(corners):
            for layer in range(SLICES):
                for part in range(2):
                    plane = (layer * 2 + part) * halves
                    rolled = pltpu.roll(grads[i][layer][part], lax.rem(c, extent), 1)
                    acc[plane, pl.ds(r, extent), :] += jnp.where(lane >= c, rolled, 0.0)
                    acc[plane + 1, pl.ds(r, extent), :] += jnp.where(lane >= c, 0.0, rolled)

    count = counts_ref[0]

    def pair(j, carry):
        run([2 * j, 2 * j + 1])
        return carry

    lax.fori_loop(0, lax.shift_right_logical(count, 1), pair, 0)

    @pl.when(lax.bitwise_and(count, 1) == 1)
    def _():
        run([count - 1])

    for layer in range(SLICES):
        for half in range(halves):
            for part in range(2):
                target = (layer * halves + half) * 2 + part
                plane = (layer * 2 + part) * halves + half
                own_out[pl.ds(target, tile_rows, stride=8), :] = acc[plane, :tile_rows]
                next_out[pl.ds(target, extent, stride=8), :] = acc[plane, tile_rows:]
    for k in range(2 * MODES):
        probe_out[pl.ds(k, extent, stride=2 * MODES), :] = probe_acc[k]


def terms(row_offsets, col_offsets, counts, own, upper, probe, patterns):
    extent = patterns.shape[1]
    rows = own.shape[0] // 8 + extent
    mats = jnp.asarray(block_matrices(extent))
    smem = pl.BlockSpec(memory_space=pltpu.SMEM)
    vmem = pl.BlockSpec(memory_space=pltpu.VMEM)
    return pl.pallas_call(
        kernel,
        out_shape=(
            jax.ShapeDtypeStruct(own.shape, jnp.float32),
            jax.ShapeDtypeStruct(upper.shape, jnp.float32),
            jax.ShapeDtypeStruct(probe.shape, jnp.float32),
        ),
        in_specs=[smem] * 3 + [vmem] * 5,
        out_specs=(vmem, vmem, vmem),
        scratch_shapes=[
            pltpu.VMEM((8, rows, extent), jnp.float32),
            pltpu.VMEM((8, rows, extent), jnp.float32),
            pltpu.VMEM((2 * MODES, extent, extent), jnp.float32),
            pltpu.VMEM((2 * MODES, extent, extent), jnp.float32),
        ],
        compiler_params=pltpu.CompilerParams(vmem_limit_bytes=40 * 1024 * 1024),
    )(row_offsets, col_offsets, counts, own, upper, probe, patterns, mats)


def flat(block):
    rows, k, parts, columns = block.shape
    split_up = block.reshape(rows, k, parts, columns // 128, 128)
    return split_up.transpose(0, 1, 3, 2, 4).reshape(-1, 128)


def unflat(value, shape):
    rows, k, parts, columns = shape
    return value.reshape(rows, k, columns // 128, parts, 128).transpose(0, 1, 3, 2, 4).reshape(shape)


def shards(object_slices, probe_field, patterns, row_offsets, col_offsets, counts):
    size = lax.axis_size("tile")
    groups = [list(range(g, g + GROUP_DEV)) for g in range(0, size, GROUP_DEV)]
    own = flat(object_slices)
    upper = lax.ppermute(own, "tile", [((i + 1) % size, i) for i in range(size)])
    probe = lax.all_gather(flat(probe_field), "tile", axis_index_groups=groups, tiled=True)
    own_grad, upper_grad, probe_grad = terms(row_offsets, col_offsets, counts, own, upper, probe, patterns)
    back = lax.ppermute(upper_grad, "tile", [(i, (i + 1) % size) for i in range(size)])
    probe_sum = lax.psum_scatter(probe_grad, "tile", axis_index_groups=groups, tiled=True)
    return unflat(own_grad + back, object_slices.shape), unflat(probe_sum, probe_field.shape)


def solution(mesh):
    in_specs = (
        P(("groups", "tile"), None, None, None),
        P(("groups", "tile"), None, None, None),
        P(("groups", "tile"), None, None),
        P(("groups", "tile")),
        P(("groups", "tile")),
        P(("groups", "tile")),
    )
    out_specs = (P(("groups", "tile"), None, None, None), P(("groups", "tile"), None, None, None))
    return jax.shard_map(shards, mesh=mesh, in_specs=in_specs, out_specs=out_specs, check_vma=False)
```

time: 1300 us -> 132 us (0.10); the launches traced: 1280 us -> 132 us
  starting transfers between devices: 589 us -> 5.51 us
  local copies, waits for them, and re-layouts: 373 us -> 3.49 us
  matrix products: 204 us -> 0 us
  loops' own time: 43.4 us -> 0 us
  other arithmetic: 29 us -> 0.85 us
  waiting for transfers between devices: 40.5 us -> 68.4 us
  blocking collectives: 0 us -> 22.8 us
  Pallas kernels: 0 us -> 16.4 us
  between operations: 0.8 us -> 14.7 us
    ppermute x10 -> x2, starting transfers between devices: 589 us -> 5.47 us  [the longest x1 5.47 us: shards(): lax.ppermute(own, 'tile', [((i + 1) % size, i) for i in range(size)])]
    dynamic_update_slice x8 -> x0, local copies, waits for them, and re-layouts: 343 us -> none  [deposit(): return lax.dynamic_update_slice(accumulated, current + patch_grad, corner)]
    dot_general x384 -> x0, matrix products: 204 us -> none  [multiply(): jnp.dot(left_side, right_side, precision=HIGHEST, preferred_element_type=...]
    reduce_scatter x0 -> x1, waiting for transfers between devices: none -> 57.1 us  [shards(): lax.psum_scatter(probe_grad, 'tile', axis_index_groups=groups, tiled=True)]
    another operation x1 -> x0, loops' own time: 43.4 us -> none  [shards(): lax.fori_loop(0, own_count, own_step, starting)]
    ppermute x10 -> x2, waiting for transfers between devices: 40.5 us -> 11.3 us  [the longest x1 11.3 us: shards(): lax.ppermute(upper_grad, 'tile', [(i, (i + 1) % size) for i in range(size)])]
    all_gather x0 -> x1, blocking collectives: none -> 22.8 us  [shards(): lax.all_gather(flat(probe_field), 'tile', axis_index_groups=groups, tiled...]
    pallas_call x0 -> x1, Pallas kernels: none -> 16.4 us  [terms(): pl.pallas_call(kernel, out_shape=(jax.ShapeDtypeStruct(own.shape, jnp.flo...]
  transfers between devices with their start and end apart: 10 -> 3, of which waited for: 7 -> 2; matrix products, arithmetic and copies ran while one was open for 0% -> 1% of each run, Pallas kernels for 0% -> 0%
where the time goes in v1:
time: 132 us
  waiting for transfers between devices  68.4 us (52%)
  blocking collectives  22.8 us (17%)
  Pallas kernels  16.4 us (12%)
  between operations  14.7 us (11%)
  starting transfers between devices  5.51 us (4%)
  local copies, waits for them, and re-layouts  3.49 us (3%)
    reduce_scatter x1, waiting for transfers between devices, shards(): lax.psum_scatter(probe_grad, 'tile', axis_index_groups=groups, tiled=True)  57.1 us
    all_gather x1, blocking collectives, shards(): lax.all_gather(flat(probe_field), 'tile', axis_index_groups=groups, tiled...  22.8 us
    pallas_call x1, Pallas kernels, terms(): pl.pallas_call(kernel, out_shape=(jax.ShapeDtypeStruct(own.shape, jnp.flo...  16.4 us
    ppermute x1, waiting for transfers between devices, shards(): lax.ppermute(upper_grad, 'tile', [(i, (i + 1) % size) for i in range(size)])  11.3 us
    ppermute x1, starting transfers between devices, shards(): lax.ppermute(own, 'tile', [((i + 1) % size, i) for i in range(size)])  5.47 us
    unnamed x10, local copies, waits for them, and re-layouts  3.49 us
  transfers between devices with their start and end apart: 3, of which 2 were waited for; matrix products, arithmetic and copies ran while one was open for 1% of the time, Pallas kernels for 0%

profile of v1, /device:TPU:0, one launch (start us, length us, event | category | flops | bytes accessed | tf_op | source)
XLA Modules:
  0.0 132.1 jit_solution(10079338269910624277)
XLA Ops:
  7.2 0.0 reduce-scatter.2.cloned.1.call-start
  7.2 5.5 %collective-permute-start = (f32[1024,128]{1,0:T(8,128)}, f32[1024,128]{1,0:T(8,128)S(1)}, u32[]{:S(2)}, u32[]{:S(2)}) collective-permute-start(f32[1024,128]{1,0:T(8,128)} %bitcast.12), channel_id=1, source_target_pairs={{1,0},{2,1},{3,2},{4,3},{5,4},{6,5},{7,6},{8,7},{9,8},{10,9},{11,1... | collective-permute-start | bytes 1572872 | tf_op jit(solution)/shard_map/ppermute | solution.py:206
  13.3 0.0 copy-start.3
  13.3 0.0 copy-start.4
  13.4 22.8 %all_gather.3.probe_ref = f32[512,128]{1,0:T(8,128)S(1)} all-gather(f32[32,128]{1,0:T(8,128)} %bitcast.15), channel_id=1, replica_groups={{0,1,2,3,4,5,6,7,8,9,10,11,12,13,14,15},{16,17,18,19,20,21,22,23,24,25,..., dimensions={0}, use_global_device_ids=true | all-gather | bytes 278528 | tf_op jit(solution)/shard_map/all_gather | solution.py:207
  36.1 0.0 collective-permute-done.next_ref
  36.1 0.0 copy-done.3
  36.1 0.0 copy-done.4
  36.1 0.0 copy-start
  36.1 1.2 copy-done
  37.4 0.0 copy-start.1
  37.4 1.2 copy-done.1
  38.6 0.0 copy-start.2
  38.6 1.0 copy-done.2
  39.6 16.4 %shard_map.86 = (f32[1024,128]{1,0:T(8,128)S(1)}, f32[1024,128]{1,0:T(8,128)S(1)}, f32[512,128]{1,0:T(8,128)}) custom-call(s32[16]{0:T(128)S(1)} %copy-done.3, s32[16]{0:T(128)S(1)} %copy-done.4, s32[1]{0:T(128)S(6)} %copy.11.counts_ref, f32[1024,128]{1,0:T(8,128)S(1)} %bitcast.13, f32[1024,128]{1,0:T(8,128)S(1)} %collective-permute-done.next_ref, ...), custom_call_target="tpu_custom_call" | custom-call | tf_op jit(solution)/shard_map/pallas_call | solution.py:172
  56.0 0.0 collective-permute-start.1
  56.0 0.0 reduce-scatter.2.cloned.1.call-update
  56.1 11.3 %collective-permute-done.1 = f32[1024,128]{1,0:T(8,128)S(1)} collective-permute-done((f32[1024,128]{1,0:T(8,128)S(1)}, f32[1024,128]{1,0:T(8,128)S(1)}, u32[]{:S(2)}, u32[]{:S(2)}) %collective-permute-start.1) | collective-permute-done | bytes 524320 | tf_op jit(solution)/shard_map/ppermute | solution.py:209
  67.3 0.8 add.5
  68.2 57.1 %reduce-scatter.2.cloned.1.call-done = f32[32,128]{1,0:T(8,128)} async-done(((f32[512,128]{1,0:T(8,128)}), f32[32,128]{1,0:T(8,128)}) %reduce-scatter.2.cloned.1.call-update) | async-done | bytes 16400 | tf_op jit(solution)/shard_map/reduce_scatter | solution.py:210
Async XLA Ops:
  7.2 118.1 %reduce-scatter.2.cloned.1.call-start = ((), (), s32[]{:S(2)}) async-start(), calls=%async_computation.1 | async-start | bytes 278528 | tf_op jit(solution)/shard_map/reduce_scatter | solution.py:210
  7.2 28.9 %collective-permute-start = (f32[1024,128]{1,0:T(8,128)}, f32[1024,128]{1,0:T(8,128)S(1)}, u32[]{:S(2)}, u32[]{:S(2)}) collective-permute-start(f32[1024,128]{1,0:T(8,128)} %bitcast.12), channel_id=1, source_target_pairs={{1,0},{2,1},{3,2},{4,3},{5,4},{6,5},{7,6},{8,7},{9,8},{10,9},{11,1... | collective-permute-start | bytes 1572872 | tf_op jit(solution)/shard_map/ppermute | solution.py:206
  13.3 22.8 %copy-start.3 = (s32[16]{0:T(128)S(1)}, s32[16]{0:T(128)}, u32[]{:S(2)}) copy-start(s32[16]{0:T(128)} %rows_ref.1) | copy-start | bytes 196
  13.3 22.8 %copy-start.4 = (s32[16]{0:T(128)S(1)}, s32[16]{0:T(128)}, u32[]{:S(2)}) copy-start(s32[16]{0:T(128)} %cols_ref.1) | copy-start | bytes 196
  36.1 1.2 copy-start
  37.4 1.2 copy-start.1
  38.6 1.0 copy-start.2
  56.0 11.3 %collective-permute-start.1 = (f32[1024,128]{1,0:T(8,128)S(1)}, f32[1024,128]{1,0:T(8,128)S(1)}, u32[]{:S(2)}, u32[]{:S(2)}) collective-permute-start(f32[1024,128]{1,0:T(8,128)S(1)} %get-tuple-element.6), channel_id=1, source_target_pairs={{0,1},{1,2},{2,3},{3,4},{4,5},{5,6},{6,7},{7,8},{8,9},{9,10},{10,1... | collective-permute-start | bytes 1572872 | tf_op jit(solution)/shard_map/ppermute | solution.py:209
Sparse Core Ops, SparseCore 0:
  56.2 69.0 reduce-scatter.1

commit v2 on v1

v2 whole, which is shorter than its diff:
```python
import math

import jax
import jax.numpy as jnp
import numpy as np
from jax import lax
from jax.experimental import pallas as pl
from jax.experimental.pallas import tpu as pltpu
from jax.sharding import PartitionSpec as P

GROUP_DEV = 16
KAPPA = 4.0
MODES = 2
SLICES = 2
HALVES = 2


def block_matrices(extent):
    counter = np.arange(extent)
    dft = np.exp(-2j * np.pi * (counter[:, None] * counter[None, :] % extent) / extent) / math.sqrt(extent)
    freq = ((counter + extent // 2) % extent - extent // 2) / extent
    prop = np.conj(dft) @ (np.exp(-1j * np.pi * KAPPA * freq**2)[:, None] * dft)
    stacked = []
    for matrix in (dft, prop):
        for imag_sign in (1.0, -1.0):
            re, im = matrix.real, imag_sign * matrix.imag
            full = np.block([[re, im], [-im, re]]).astype(np.float32)
            high = full.astype(jnp.bfloat16)
            low = (full - high.astype(np.float32)).astype(jnp.bfloat16)
            stacked += [high, low]
    return np.stack(stacked)


def prepare(own_ref, patterns_ref, mats_ref, planes_out, patterns_out, mats_out):
    rows = planes_out.shape[1]
    for layer in range(SLICES):
        for half in range(HALVES):
            for part in range(2):
                source = (layer * HALVES + half) * 2 + part
                plane = (layer * 2 + part) * HALVES + half
                planes_out[plane] = own_ref[pl.ds(source, rows, stride=8), :]
    patterns_out[...] = patterns_ref[...]
    mats_out[...] = mats_ref[...]


def split(value):
    high = value.astype(jnp.bfloat16)
    low = (value - high.astype(jnp.float32)).astype(jnp.bfloat16)
    return high, low


def times(a, b):
    return [a[0] * b[0] - a[1] * b[1], a[0] * b[1] + a[1] * b[0]]


def conj_times(a, b):
    return [a[0] * b[0] + a[1] * b[1], a[0] * b[1] - a[1] * b[0]]


def add(a, b):
    return [a[0] + b[0], a[1] + b[1]]


def kernel(rows_ref, cols_ref, counts_ref, own_ref, next_ref, near_ref, far_ref, patterns_ref, mats_ref,
           own_out, next_out, keep_out, send_out, obj, acc, probe, probe_acc):
    extent = patterns_ref.shape[1]
    tile_rows = own_ref.shape[1]
    share = extent // GROUP_DEV
    lanes = 2 * MODES
    block = share * lanes
    member = lax.rem(lax.axis_index("tile"), GROUP_DEV)

    def member_rows(order, odd):
        bits = odd + 2 * (order // 4) + 4 * (order % 4)
        return pl.ds(pl.multiple_of(lax.bitwise_xor(member, bits) * share, share), share)

    for layer in range(SLICES):
        for half in range(HALVES):
            for part in range(2):
                source = (layer * HALVES + half) * 2 + part
                plane = (layer * 2 + part) * HALVES + half
                obj[plane, :tile_rows] = own_ref[plane]
                obj[plane, tile_rows:] = next_ref[pl.ds(source, extent, stride=8), :]
    for odd, ref in enumerate((near_ref, far_ref)):
        for order in range(GROUP_DEV // 2):
            for k in range(lanes):
                probe[k, member_rows(order, odd), :] = ref[pl.ds(order * block + k, share, stride=lanes), :]
    acc[...] = jnp.zeros(acc.shape, jnp.float32)
    probe_acc[...] = jnp.zeros(probe_acc.shape, jnp.float32)

    def right(field, kind, conj):
        high_m, low_m = mats_ref[4 * kind + 2 * conj], mats_ref[4 * kind + 2 * conj + 1]
        rows = jnp.concatenate([jnp.concatenate(field[m], axis=1) for m in range(MODES)], axis=0)
        high, low = split(rows)
        out = jnp.dot(jnp.concatenate([high, low, high], axis=1), jnp.concatenate([high_m, high_m, low_m], axis=0),
                      preferred_element_type=jnp.float32)
        return [[out[m * extent:(m + 1) * extent, c * extent:(c + 1) * extent] for c in range(2)]
                for m in range(MODES)]

    def left(field, kind, conj):
        high_m, low_m = mats_ref[4 * kind + 2 * (1 - conj)], mats_ref[4 * kind + 2 * (1 - conj) + 1]
        cols = jnp.concatenate([jnp.concatenate(field[m], axis=0) for m in range(MODES)], axis=1)
        high, low = split(cols)
        out = jnp.dot(jnp.concatenate([high_m, high_m, low_m], axis=1), jnp.concatenate([high, low, high], axis=0),
                      preferred_element_type=jnp.float32)
        return [[out[c * extent:(c + 1) * extent, m * extent:(m + 1) * extent] for c in range(2)]
                for m in range(MODES)]

    lane = lax.broadcasted_iota(jnp.int32, (extent, extent), 1)
    modes = range(MODES)

    def window(slot):
        r, c = rows_ref[slot], cols_ref[slot]
        shift = lax.rem(extent - c, extent)
        layers = []
        for layer in range(SLICES):
            parts = []
            for part in range(2):
                plane = (layer * 2 + part) * HALVES
                joined = jnp.where(lane >= c, obj[plane, pl.ds(r, extent), :], obj[plane + 1, pl.ds(r, extent), :])
                parts.append(pltpu.roll(joined, shift, 1))
            layers.append(parts)
        return layers

    def deposit(slot, layer, grad):
        r, c = rows_ref[slot], cols_ref[slot]
        for part in range(2):
            plane = (layer * 2 + part) * HALVES
            rolled = pltpu.roll(grad[part], lax.rem(c, extent), 1)
            acc[plane, pl.ds(r, extent), :] += jnp.where(lane >= c, rolled, 0.0)
            acc[plane + 1, pl.ds(r, extent), :] += jnp.where(lane >= c, 0.0, rolled)

    def steps(slot):
        field = [[probe[2 * m], probe[2 * m + 1]] for m in modes]
        objects = window(slot)
        state = right([times(field[m], objects[0]) for m in modes], 1, 0)
        yield
        entering = left(state, 1, 0)
        yield
        state = right([times(entering[m], objects[1]) for m in modes], 0, 0)
        yield
        state = left(state, 0, 0)
        yield
        intensity = sum(state[m][c] * state[m][c] for m in modes for c in range(2))
        weight = 2.0 * (intensity - patterns_ref[slot])
        state = right([[weight * state[m][c] for c in range(2)] for m in modes], 0, 1)
        yield
        state = left(state, 0, 1)
        yield
        grad = conj_times(entering[0], state[0])
        for m in modes[1:]:
            grad = add(grad, conj_times(entering[m], state[m]))
        deposit(slot, 1, grad)
        state = right([conj_times(objects[1], state[m]) for m in modes], 1, 1)
        yield
        state = left(state, 1, 1)
        yield
        grad = conj_times(field[0], state[0])
        for m in modes[1:]:
            grad = add(grad, conj_times(field[m], state[m]))
        deposit(slot, 0, grad)
        for m in modes:
            term = conj_times(objects[0], state[m])
            probe_acc[2 * m] += term[0]
            probe_acc[2 * m + 1] += term[1]

    def run(slots):
        running = [steps(slot) for slot in slots]
        while running:
            running = [r for r in running if next(r, "done") is None]

    count = counts_ref[0]

    def pair(j, carry):
        run([2 * j, 2 * j + 1])
        return carry

    lax.fori_loop(0, lax.shift_right_logical(count, 1), pair, 0)

    @pl.when(lax.bitwise_and(count, 1) == 1)
    def _():
        run([count - 1])

    for layer in range(SLICES):
        for half in range(HALVES):
            for part in range(2):
                target = (layer * HALVES + half) * 2 + part
                plane = (layer * 2 + part) * HALVES + half
                own_out[pl.ds(target, tile_rows, stride=8), :] = acc[plane, :tile_rows]
                next_out[pl.ds(target, extent, stride=8), :] = acc[plane, tile_rows:]
    for odd, ref in enumerate((keep_out, send_out)):
        for order in range(GROUP_DEV // 2):
            for k in range(lanes):
                ref[pl.ds(order * block + k, share, stride=lanes), :] = probe_acc[k, member_rows(order, odd), :]


def prepared(own, patterns):
    vmem = pl.BlockSpec(memory_space=pltpu.VMEM)
    mats = jnp.asarray(block_matrices(patterns.shape[1]))
    return pl.pallas_call(
        prepare,
        out_shape=(
            jax.ShapeDtypeStruct((8, own.shape[0] // 8, own.shape[1]), jnp.float32),
            jax.ShapeDtypeStruct(patterns.shape, jnp.float32),
            jax.ShapeDtypeStruct(mats.shape, mats.dtype),
        ),
        in_specs=[vmem] * 3,
        out_specs=(vmem,) * 3,
        compiler_params=pltpu.CompilerParams(vmem_limit_bytes=16 * 1024 * 1024),
        cost_estimate=pl.CostEstimate(flops=0, bytes_accessed=6 * 1024 * 1024, transcendentals=0),
    )(own, patterns, mats)


def terms(row_offsets, col_offsets, counts, planes, upper, near, far, patterns, mats):
    extent = patterns.shape[1]
    rows = planes.shape[1] + extent
    smem = pl.BlockSpec(memory_space=pltpu.SMEM)
    vmem = pl.BlockSpec(memory_space=pltpu.VMEM)
    return pl.pallas_call(
        kernel,
        out_shape=(
            jax.ShapeDtypeStruct((planes.shape[1] * 8, extent), jnp.float32),
            jax.ShapeDtypeStruct(upper.shape, jnp.float32),
            jax.ShapeDtypeStruct(near.shape, jnp.float32),
            jax.ShapeDtypeStruct(near.shape, jnp.float32),
        ),
        in_specs=[smem] * 3 + [vmem] * 6,
        out_specs=(vmem,) * 4,
        scratch_shapes=[
            pltpu.VMEM((8, rows, extent), jnp.float32),
            pltpu.VMEM((8, rows, extent), jnp.float32),
            pltpu.VMEM((2 * MODES, extent, extent), jnp.float32),
            pltpu.VMEM((2 * MODES, extent, extent), jnp.float32),
        ],
        compiler_params=pltpu.CompilerParams(vmem_limit_bytes=40 * 1024 * 1024),
    )(row_offsets, col_offsets, counts, planes, upper, near, far, patterns, mats)


def flat(block):
    rows, k, parts, columns = block.shape
    split_up = block.reshape(rows, k, parts, columns // 128, 128)
    return split_up.transpose(0, 1, 3, 2, 4).reshape(-1, 128)


def unflat(value, shape):
    rows, k, parts, columns = shape
    return value.reshape(rows, k, columns // 128, parts, 128).transpose(0, 1, 3, 2, 4).reshape(shape)


def partner(value, bits):
    return lax.ppermute(value, "tile", [(i, i ^ bits) for i in range(lax.axis_size("tile"))])


def gathered(own):
    quarter = jnp.concatenate([own] + [partner(own, 4 * k) for k in range(1, 4)], axis=0)
    near = jnp.concatenate([quarter, partner(quarter, 2)], axis=0)
    return near, partner(near, 1)


def scattered(keep, send):
    total = keep + partner(send, 1)
    half = total.shape[0] // 2
    total = total[:half] + partner(total[half:], 2)
    parts = jnp.split(total, 4, axis=0)
    return parts[0] + (partner(parts[1], 4) + partner(parts[2], 8) + partner(parts[3], 12))


def shards(object_slices, probe_field, patterns, row_offsets, col_offsets, counts):
    size = lax.axis_size("tile")
    own = flat(object_slices)
    upper = lax.ppermute(own, "tile", [((i + 1) % size, i) for i in range(size)])
    near, far = gathered(flat(probe_field))
    planes, patterns, mats = prepared(own, patterns)
    own_grad, upper_grad, keep, send = terms(
        row_offsets, col_offsets, counts, planes, upper, near, far, patterns, mats)
    back = lax.ppermute(upper_grad, "tile", [(i, (i + 1) % size) for i in range(size)])
    probe_sum = scattered(keep, send)
    return unflat(own_grad + back, object_slices.shape), unflat(probe_sum, probe_field.shape)


def solution(mesh):
    in_specs = (
        P(("groups", "tile"), None, None, None),
        P(("groups", "tile"), None, None, None),
        P(("groups", "tile"), None, None),
        P(("groups", "tile")),
        P(("groups", "tile")),
        P(("groups", "tile")),
    )
    out_specs = (P(("groups", "tile"), None, None, None), P(("groups", "tile"), None, None, None))
    return jax.shard_map(shards, mesh=mesh, in_specs=in_specs, out_specs=out_specs, check_vma=False)
```

time: 132 us -> 65.6 us (0.50)
  waiting for transfers between devices: 68.4 us -> 15.2 us
  starting transfers between devices: 5.51 us -> 29.7 us
  blocking collectives: 22.8 us -> 0 us
  between operations: 14.7 us -> 1.39 us
  Pallas kernels: 16.4 us -> 14.1 us
  local copies, waits for them, and re-layouts: 3.49 us -> 4.89 us
    reduce_scatter x1 -> x0, waiting for transfers between devices: 57.1 us -> none  [shards(): lax.psum_scatter(probe_grad, 'tile', axis_index_groups=groups, tiled=True)]
    ppermute x0 -> x10, starting transfers between devices: none -> 26.2 us  [partner(): lax.ppermute(value, 'tile', [(i, i ^ bits) for i in range(lax.axis_size('...]
    all_gather x1 -> x0, blocking collectives: 22.8 us -> none  [shards(): lax.all_gather(flat(probe_field), 'tile', axis_index_groups=groups, tiled...]
    ppermute x0 -> x10, waiting for transfers between devices: none -> 15.2 us  [partner(): lax.ppermute(value, 'tile', [(i, i ^ bits) for i in range(lax.axis_size('...]
    ppermute x1, waiting for transfers between devices: 11.3 us -> 0.01 us  [shards(): lax.ppermute(upper_grad, 'tile', [(i, (i + 1) % size) for i in range(size)])]
    pallas_call x1 -> x2, Pallas kernels: 16.4 us -> 14.1 us  [the longest x1 13.9 us: terms(): pl.pallas_call(kernel, out_shape=(jax.ShapeDtypeStruct((planes.shape[1] *...]
    ppermute x1, starting transfers between devices: 5.47 us -> 3.27 us  [shards(): lax.ppermute(own, 'tile', [((i + 1) % size, i) for i in range(size)])]
    unnamed x10 -> x16, local copies, waits for them, and re-layouts: 3.49 us -> 4.87 us
  transfers between devices with their start and end apart: 3 -> 12, of which waited for: 2 -> 6; matrix products, arithmetic and copies ran while one was open for 1% -> 2% of each run, Pallas kernels for 0% -> 0%
where the time goes in v2:
time: 65.6 us; the launch traced here: 66.8 us
  starting transfers between devices  29.7 us (45%)
  waiting for transfers between devices  15.2 us (23%)
  Pallas kernels  14.1 us (21%)
  local copies, waits for them, and re-layouts  4.89 us (7%)
  other arithmetic  1.49 us (2%)
  between operations  1.39 us (2%)
    ppermute x10, starting transfers between devices, partner(): lax.ppermute(value, 'tile', [(i, i ^ bits) for i in range(lax.axis_size('...  26.2 us
    ppermute x10, waiting for transfers between devices, partner(): lax.ppermute(value, 'tile', [(i, i ^ bits) for i in range(lax.axis_size('...  15.2 us
    pallas_call x1, Pallas kernels, terms(): pl.pallas_call(kernel, out_shape=(jax.ShapeDtypeStruct((planes.shape[1] *...  13.9 us
    unnamed x16, local copies, waits for them, and re-layouts  4.87 us
    ppermute x1, starting transfers between devices, shards(): lax.ppermute(own, 'tile', [((i + 1) % size, i) for i in range(size)])  3.27 us
  transfers between devices with their start and end apart: 12, of which 6 were waited for; matrix products, arithmetic and copies ran while one was open for 2% of the time, Pallas kernels for 0%

profile of v2, /device:TPU:0, one launch (start us, length us, event | category | flops | bytes accessed | tf_op | source)
XLA Modules:
  0.0 66.8 jit_solution(304607712202745398)
XLA Ops:
  0.6 5.1 %collective-permute-start.3 = (f32[32,128]{1,0:T(8,128)}, f32[32,128]{1,0:T(8,128)S(1)}, u32[]{:S(2)}, u32[]{:S(2)}) collective-permute-start(f32[32,128]{1,0:T(8,128)} %bitcast.15), channel_id=1, source_target_pairs={{0,12},{1,13},{2,14},{3,15},{4,8},{5,9},{6,10},{7,11},{8,4},{9,5},... | collective-permute-start | bytes 49160 | tf_op jit(solution)/shard_map/ppermute | solution.py:251
  5.7 0.0 collective-permute-start.2
  5.7 0.6 collective-permute-start.1
  6.4 0.0 copy-start.5
  6.4 3.3 %collective-permute-start = (f32[1024,128]{1,0:T(8,128)}, f32[1024,128]{1,0:T(8,128)S(1)}, u32[]{:S(2)}, u32[]{:S(2)}) collective-permute-start(f32[1024,128]{1,0:T(8,128)} %bitcast.12), channel_id=1, source_target_pairs={{1,0},{2,1},{3,2},{4,3},{5,4},{6,5},{7,6},{8,7},{9,8},{10,9},{11,1... | collective-permute-start | bytes 1572872 | tf_op jit(solution)/shard_map/ppermute | solution.py:271
  9.7 0.7 %constant_dynamic-update-slice_fusion.4 = f32[256,128]{1,0:T(8,128)S(1)} fusion(f32[32,128]{1,0:T(8,128)} %bitcast.18), kind=kLoop, calls=%fused_computation.7 | loop fusion | bytes 32768
  10.4 0.0 collective-permute-done.3
  10.4 0.3 collective-permute-done.2
  10.7 0.0 collective-permute-done.1
  10.7 0.0 copy-done.5
  10.7 1.5 %collective-permute-start.4 = (f32[128,128]{1,0:T(8,128)S(1)}, f32[128,128]{1,0:T(8,128)S(1)}, u32[]{:S(2)}, u32[]{:S(2)}) collective-permute-start(f32[128,128]{1,0:T(8,128)S(1)} %pad_maximum_fusion), channel_id=1, source_target_pairs={{0,2},{1,3},{2,0},{3,1},{4,6},{5,7},{6,4},{7,5},{8,10},{9,11},{10,... | collective-permute-start | bytes 196616 | tf_op jit(solution)/shard_map/ppermute | solution.py:251
  12.2 4.6 %collective-permute-done.4 = f32[128,128]{1,0:T(8,128)S(1)} collective-permute-done((f32[128,128]{1,0:T(8,128)S(1)}, f32[128,128]{1,0:T(8,128)S(1)}, u32[]{:S(2)}, u32[]{:S(2)}) %collective-permute-start.4) | collective-permute-done | bytes 65568 | tf_op jit(solution)/shard_map/ppermute | solution.py:251
  16.8 0.0 collective-permute-start.5
  17.5 0.0 copy-start
  17.5 1.2 %copy-done = f32[16,128,128]{2,1,0:T(8,128)S(1)} copy-done((f32[16,128,128]{2,1,0:T(8,128)S(1)}, f32[16,128,128]{2,1,0:T(8,128)}, u32[]{:S(2)}) %copy-start) | copy-done | bytes 1048600
  18.7 0.0 copy-start.1
  18.7 1.2 %copy-done.1 = bf16[8,256,256]{2,1,0:T(8,128)(2,1)S(1)} copy-done((bf16[8,256,256]{2,1,0:T(8,128)(2,1)S(1)}, bf16[8,256,256]{2,1,0:T(8,128)(2,1)}, u32[]{:S(2)}) %copy-start.1) | copy-done | bytes 1048600
  19.9 0.0 copy-start.2
  19.9 1.0 %copy-done.2 = f32[128,2,2,256]{3,2,1,0:T(2,128)S(1)} copy-done((f32[128,2,2,256]{3,2,1,0:T(2,128)S(1)}, f32[128,2,2,256]{3,2,1,0:T(2,128)}, u32[]{:S(2)}) %copy-start.2) | copy-done | bytes 524312
  21.0 0.2 shard_map.86
  21.2 0.0 collective-permute-done.5.far_ref
  21.2 0.0 collective-permute-done.next_ref
  21.2 0.0 copy-start.3
  21.2 0.0 copy-start.4
  21.2 0.6 copy-done.3
  21.9 0.0 copy-done.4
  21.9 13.9 %shard_map.87 = (f32[1024,128]{1,0:T(8,128)S(1)}, f32[1024,128]{1,0:T(8,128)S(1)}, f32[256,128]{1,0:T(8,128)S(1)}, f32[256,128]{1,0:T(8,128)S(1)}) custom-call(s32[16]{0:T(128)S(1)} %copy-done.3, s32[16]{0:T(128)S(1)} %copy-done.4, s32[1]{0:T(128)S(6)} %copy.15.counts_ref, f32[8,128,128]{2,1,0:T(8,128)S(1)} %get-tuple-element.9.own_ref, ...), custom_call_target="tpu_custom_call" | custom-call | tf_op jit(solution)/shard_map/pallas_call | solution.py:219
  35.8 0.1 collective-permute-start.7
  35.9 1.3 %collective-permute-done.7 = f32[256,128]{1,0:T(8,128)S(1)} collective-permute-done((f32[256,128]{1,0:T(8,128)S(1)}, f32[256,128]{1,0:T(8,128)S(1)}, u32[]{:S(2)}, u32[]{:S(2)}) %collective-permute-start.7) | collective-permute-done | bytes 131104 | tf_op jit(solution)/shard_map/ppermute | solution.py:251
  37.2 0.1 collective-permute-start.8
  37.3 0.2 collective-permute-start.6
  37.5 4.1 %collective-permute-done.8 = f32[128,128]{1,0:T(8,128)S(1)} collective-permute-done((f32[128,128]{1,0:T(8,128)S(1)}, f32[128,128]{1,0:T(8,128)S(1)}, u32[]{:S(2)}, u32[]{:S(2)}) %collective-permute-start.8) | collective-permute-done | bytes 65568 | tf_op jit(solution)/shard_map/ppermute | solution.py:251
  41.6 18.2 %collective-permute-start.10 = (f32[32,128]{1,0:T(8,128)S(1)}, f32[32,128]{1,0:T(8,128)S(1)}, u32[]{:S(2)}, u32[]{:S(2)}) collective-permute-start(f32[32,128]{1,0:T(8,128)S(1)} %get-tuple-element.16), channel_id=1, source_target_pairs={{0,8},{1,9},{2,10},{3,11},{4,12},{5,13},{6,14},{7,15},{8,0},{9,1},... | collective-permute-start | bytes 49160 | tf_op jit(solution)/shard_map/ppermute | solution.py:251
  59.8 0.0 collective-permute-start.11
  59.8 0.6 collective-permute-start.9
  60.5 1.1 %collective-permute-done.10 = f32[32,128]{1,0:T(8,128)S(1)} collective-permute-done((f32[32,128]{1,0:T(8,128)S(1)}, f32[32,128]{1,0:T(8,128)S(1)}, u32[]{:S(2)}, u32[]{:S(2)}) %collective-permute-start.10) | collective-permute-done | bytes 16416 | tf_op jit(solution)/shard_map/ppermute | solution.py:251
  61.5 3.8 %collective-permute-done.11 = f32[32,128]{1,0:T(8,128)S(1)} collective-permute-done((f32[32,128]{1,0:T(8,128)S(1)}, f32[32,128]{1,0:T(8,128)S(1)}, u32[]{:S(2)}, u32[]{:S(2)}) %collective-permute-start.11) | collective-permute-done | bytes 16416 | tf_op jit(solution)/shard_map/ppermute | solution.py:251
  65.4 0.0 collective-permute-done.9
  65.4 0.6 slice_add_fusion.1
  66.0 0.0 collective-permute-done.6
  66.0 0.8 %add.18 = f32[1024,128]{1,0:T(8,128)} add(f32[1024,128]{1,0:T(8,128)S(1)} %get-tuple-element.12, f32[1024,128]{1,0:T(8,128)S(1)} %collective-permute-done.6) | non-fusion elementwise | flops 131072 | bytes 1572864 | tf_op jit(solution)/shard_map/add | solution.py:278
  (9 shorter events, 0.1 us)
Async XLA Ops:
  0.6 9.8 %collective-permute-start.3 = (f32[32,128]{1,0:T(8,128)}, f32[32,128]{1,0:T(8,128)S(1)}, u32[]{:S(2)}, u32[]{:S(2)}) collective-permute-start(f32[32,128]{1,0:T(8,128)} %bitcast.15), channel_id=1, source_target_pairs={{0,12},{1,13},{2,14},{3,15},{4,8},{5,9},{6,10},{7,11},{8,4},{9,5},... | collective-permute-start | bytes 49160 | tf_op jit(solution)/shard_map/ppermute | solution.py:251
  5.7 4.9 %collective-permute-start.2 = (f32[32,128]{1,0:T(8,128)}, f32[32,128]{1,0:T(8,128)S(1)}, u32[]{:S(2)}, u32[]{:S(2)}) collective-permute-start(f32[32,128]{1,0:T(8,128)} %bitcast.16), channel_id=1, source_target_pairs={{0,8},{1,9},{2,10},{3,11},{4,12},{5,13},{6,14},{7,15},{8,0},{9,1},... | collective-permute-start | bytes 49160 | tf_op jit(solution)/shard_map/ppermute | solution.py:251
  5.7 4.9 %collective-permute-start.1 = (f32[32,128]{1,0:T(8,128)}, f32[32,128]{1,0:T(8,128)S(1)}, u32[]{:S(2)}, u32[]{:S(2)}) collective-permute-start(f32[32,128]{1,0:T(8,128)} %bitcast.17), channel_id=1, source_target_pairs={{0,4},{1,5},{2,6},{3,7},{4,0},{5,1},{6,2},{7,3},{8,12},{9,13},{10,... | collective-permute-start | bytes 49160 | tf_op jit(solution)/shard_map/ppermute | solution.py:251
  6.4 4.3 %copy-start.5 = (f32[8,2,2,128]{3,2,1,0:T(2,128)S(1)}, f32[8,2,2,128]{3,2,1,0:T(2,128)}, u32[]{:S(2)}) copy-start(f32[8,2,2,128]{3,2,1,0:T(2,128)} %param.8) | copy-start | bytes 49156
  6.4 14.8 %collective-permute-start = (f32[1024,128]{1,0:T(8,128)}, f32[1024,128]{1,0:T(8,128)S(1)}, u32[]{:S(2)}, u32[]{:S(2)}) collective-permute-start(f32[1024,128]{1,0:T(8,128)} %bitcast.12), channel_id=1, source_target_pairs={{1,0},{2,1},{3,2},{4,3},{5,4},{6,5},{7,6},{8,7},{9,8},{10,9},{11,1... | collective-permute-start | bytes 1572872 | tf_op jit(solution)/shard_map/ppermute | solution.py:271
  10.7 6.1 %collective-permute-start.4 = (f32[128,128]{1,0:T(8,128)S(1)}, f32[128,128]{1,0:T(8,128)S(1)}, u32[]{:S(2)}, u32[]{:S(2)}) collective-permute-start(f32[128,128]{1,0:T(8,128)S(1)} %pad_maximum_fusion), channel_id=1, source_target_pairs={{0,2},{1,3},{2,0},{3,1},{4,6},{5,7},{6,4},{7,5},{8,10},{9,11},{10,... | collective-permute-start | bytes 196616 | tf_op jit(solution)/shard_map/ppermute | solution.py:251
  16.8 4.4 %collective-permute-start.5 = (f32[256,128]{1,0:T(8,128)S(1)}, f32[256,128]{1,0:T(8,128)S(1)}, u32[]{:S(2)}, u32[]{:S(2)}) collective-permute-start(f32[256,128]{1,0:T(8,128)S(1)} %constant_dynamic-update-slice_fusion.near_ref), channel_id=1, source_target_pairs={{0,1},{1,0},{2,3},{3,2},{4,5},{5,4},{6,7},{7,6},{8,9},{9,8},{10,11... | collective-permute-start | bytes 393224 | tf_op jit(solution)/shard_map/ppermute | solution.py:251
  17.5 1.2 %copy-start = (f32[16,128,128]{2,1,0:T(8,128)S(1)}, f32[16,128,128]{2,1,0:T(8,128)}, u32[]{:S(2)}) copy-start(f32[16,128,128]{2,1,0:T(8,128)} %patterns_ref.1) | copy-start | bytes 3145732
  18.7 1.2 %copy-start.1 = (bf16[8,256,256]{2,1,0:T(8,128)(2,1)S(1)}, bf16[8,256,256]{2,1,0:T(8,128)(2,1)}, u32[]{:S(2)}) copy-start(bf16[8,256,256]{2,1,0:T(8,128)(2,1)} %constant.2.clone.mats_ref) | copy-start | bytes 3145732
  19.9 1.0 %copy-start.2 = (f32[128,2,2,256]{3,2,1,0:T(2,128)S(1)}, f32[128,2,2,256]{3,2,1,0:T(2,128)}, u32[]{:S(2)}) copy-start(f32[128,2,2,256]{3,2,1,0:T(2,128)} %param.7) | copy-start | bytes 1572868
  21.2 0.7 copy-start.3
  21.2 0.7 copy-start.4
  35.8 1.4 %collective-permute-start.7 = (f32[256,128]{1,0:T(8,128)S(1)}, f32[256,128]{1,0:T(8,128)S(1)}, u32[]{:S(2)}, u32[]{:S(2)}) collective-permute-start(f32[256,128]{1,0:T(8,128)S(1)} %get-tuple-element.15), channel_id=1, source_target_pairs={{0,1},{1,0},{2,3},{3,2},{4,5},{5,4},{6,7},{7,6},{8,9},{9,8},{10,11... | collective-permute-start | bytes 393224 | tf_op jit(solution)/shard_map/ppermute | solution.py:251
  37.2 4.3 %collective-permute-start.8 = (f32[128,128]{1,0:T(8,128)S(1)}, f32[128,128]{1,0:T(8,128)S(1)}, u32[]{:S(2)}, u32[]{:S(2)}) collective-permute-start(f32[128,128]{1,0:T(8,128)S(1)} %slice.9), channel_id=1, source_target_pairs={{0,2},{1,3},{2,0},{3,1},{4,6},{5,7},{6,4},{7,5},{8,10},{9,11},{10,... | collective-permute-start | bytes 196616 | tf_op jit(solution)/shard_map/ppermute | solution.py:251
  37.3 28.7 %collective-permute-start.6 = (f32[1024,128]{1,0:T(8,128)S(1)}, f32[1024,128]{1,0:T(8,128)S(1)}, u32[]{:S(2)}, u32[]{:S(2)}) collective-permute-start(f32[1024,128]{1,0:T(8,128)S(1)} %get-tuple-element.13), channel_id=1, source_target_pairs={{0,1},{1,2},{2,3},{3,4},{4,5},{5,6},{6,7},{7,8},{8,9},{9,10},{10,1... | collective-permute-start | bytes 1572872 | tf_op jit(solution)/shard_map/ppermute | solution.py:276
  41.6 19.9 %collective-permute-start.10 = (f32[32,128]{1,0:T(8,128)S(1)}, f32[32,128]{1,0:T(8,128)S(1)}, u32[]{:S(2)}, u32[]{:S(2)}) collective-permute-start(f32[32,128]{1,0:T(8,128)S(1)} %get-tuple-element.16), channel_id=1, source_target_pairs={{0,8},{1,9},{2,10},{3,11},{4,12},{5,13},{6,14},{7,15},{8,0},{9,1},... | collective-permute-start | bytes 49160 | tf_op jit(solution)/shard_map/ppermute | solution.py:251
  59.8 5.5 %collective-permute-start.11 = (f32[32,128]{1,0:T(8,128)S(1)}, f32[32,128]{1,0:T(8,128)S(1)}, u32[]{:S(2)}, u32[]{:S(2)}) collective-permute-start(f32[32,128]{1,0:T(8,128)S(1)} %get-tuple-element.17), channel_id=1, source_target_pairs={{0,12},{1,13},{2,14},{3,15},{4,8},{5,9},{6,10},{7,11},{8,4},{9,5},... | collective-permute-start | bytes 49160 | tf_op jit(solution)/shard_map/ppermute | solution.py:251
  59.8 5.5 %collective-permute-start.9 = (f32[32,128]{1,0:T(8,128)S(1)}, f32[32,128]{1,0:T(8,128)S(1)}, u32[]{:S(2)}, u32[]{:S(2)}) collective-permute-start(f32[32,128]{1,0:T(8,128)S(1)} %get-tuple-element.18), channel_id=1, source_target_pairs={{0,4},{1,5},{2,6},{3,7},{4,0},{5,1},{6,2},{7,3},{8,12},{9,13},{10,... | collective-permute-start | bytes 49160 | tf_op jit(solution)/shard_map/ppermute | solution.py:251

commit v3 on v2

v3 whole, which is shorter than its diff:
```python
import math

import jax
import jax.numpy as jnp
import numpy as np
from jax import lax
from jax.experimental import pallas as pl
from jax.experimental.pallas import tpu as pltpu
from jax.sharding import PartitionSpec as P

GROUP_DEV = 16
KAPPA = 4.0
MODES = 2
SLICES = 2
HALVES = 2


def factors(extent):
    counter = np.arange(extent)
    dft = np.exp(-2j * np.pi * (counter[:, None] * counter[None, :] % extent) / extent) / math.sqrt(extent)
    freq = ((counter + extent // 2) % extent - extent // 2) / extent
    prop = np.conj(dft) @ (np.exp(-1j * np.pi * KAPPA * freq**2)[:, None] * dft)
    return np.stack([part for matrix in (dft, prop) for part in (matrix.real, matrix.imag)]).astype(np.float32)


def split(value):
    high = value.astype(jnp.bfloat16)
    low = (value - high.astype(jnp.float32)).astype(jnp.bfloat16)
    return high, low


def prepare(own_ref, patterns_ref, factors_ref, planes_out, patterns_out, mats_out, own, parts, sems):
    copies = [pltpu.make_async_copy(source, target, sems.at[i]) for i, (source, target) in enumerate(
        ((factors_ref, parts), (own_ref, own), (patterns_ref, patterns_out)))]
    for copy in copies:
        copy.start()
    copies[0].wait()
    extent = parts.shape[1]
    for kind in range(2):
        real, imag = split(parts[2 * kind]), split(parts[2 * kind + 1])
        for conj in range(2):
            for k in range(2):
                mat = 4 * kind + 2 * conj + k
                upper, lower = (-imag[k], imag[k]) if conj else (imag[k], -imag[k])
                mats_out[mat, :extent, :extent] = real[k]
                mats_out[mat, :extent, extent:] = upper
                mats_out[mat, extent:, :extent] = lower
                mats_out[mat, extent:, extent:] = real[k]
    copies[1].wait()
    rows = planes_out.shape[1]
    for layer in range(SLICES):
        for half in range(HALVES):
            for part in range(2):
                source = (layer * HALVES + half) * 2 + part
                plane = (layer * 2 + part) * HALVES + half
                planes_out[plane] = own[pl.ds(source, rows, stride=8), :]
    copies[2].wait()


def times(a, b):
    return [a[0] * b[0] - a[1] * b[1], a[0] * b[1] + a[1] * b[0]]


def conj_times(a, b):
    return [a[0] * b[0] + a[1] * b[1], a[0] * b[1] - a[1] * b[0]]


def add(a, b):
    return [a[0] + b[0], a[1] + b[1]]


def kernel(scalars_ref, own_ref, next_ref, probe_ref, patterns_ref, mats_ref,
           own_out, next_out, probe_out, obj, acc, probe, probe_acc):
    most, extent = patterns_ref.shape[:2]
    tile_rows = own_ref.shape[1]
    lanes = 2 * MODES
    modes = range(MODES)

    for layer in range(SLICES):
        for half in range(HALVES):
            for part in range(2):
                source = (layer * HALVES + half) * 2 + part
                plane = (layer * 2 + part) * HALVES + half
                obj[plane, :tile_rows] = own_ref[plane]
                obj[plane, tile_rows:] = next_ref[pl.ds(source, extent, stride=8), :]
    for k in range(lanes):
        probe[k] = probe_ref[pl.ds(k, extent, stride=lanes), :]
    acc[...] = jnp.zeros(acc.shape, jnp.float32)
    probe_acc[...] = jnp.zeros(probe_acc.shape, jnp.float32)

    def right(fields, kind, conj):
        high_m, low_m = mats_ref[4 * kind + 2 * conj], mats_ref[4 * kind + 2 * conj + 1]
        rows = jnp.concatenate([jnp.concatenate(f[m], axis=1) for f in fields for m in modes], axis=0)
        high, low = split(rows)
        out = jnp.dot(jnp.concatenate([high, low, high], axis=1), jnp.concatenate([high_m, high_m, low_m], axis=0),
                      preferred_element_type=jnp.float32)
        return [[[out[(i * MODES + m) * extent:(i * MODES + m + 1) * extent, c * extent:(c + 1) * extent]
                  for c in range(2)] for m in modes] for i in range(len(fields))]

    def left(fields, kind, conj):
        high_m, low_m = mats_ref[4 * kind + 2 * (1 - conj)], mats_ref[4 * kind + 2 * (1 - conj) + 1]
        cols = jnp.concatenate([jnp.concatenate(f[m], axis=0) for f in fields for m in modes], axis=1)
        high, low = split(cols)
        out = jnp.dot(jnp.concatenate([high_m, high_m, low_m], axis=1), jnp.concatenate([high, low, high], axis=0),
                      preferred_element_type=jnp.float32)
        return [[[out[c * extent:(c + 1) * extent, (i * MODES + m) * extent:(i * MODES + m + 1) * extent]
                  for c in range(2)] for m in modes] for i in range(len(fields))]

    lane = lax.broadcasted_iota(jnp.int32, (extent, extent), 1)

    def window(slot):
        r, c = scalars_ref[slot], scalars_ref[most + slot]
        shift = lax.rem(extent - c, extent)
        layers = []
        for layer in range(SLICES):
            parts = []
            for part in range(2):
                plane = (layer * 2 + part) * HALVES
                joined = jnp.where(lane >= c, obj[plane, pl.ds(r, extent), :], obj[plane + 1, pl.ds(r, extent), :])
                parts.append(pltpu.roll(joined, shift, 1))
            layers.append(parts)
        return layers

    def deposit(slot, layer, grad):
        r, c = scalars_ref[slot], scalars_ref[most + slot]
        for part in range(2):
            plane = (layer * 2 + part) * HALVES
            rolled = pltpu.roll(grad[part], lax.rem(c, extent), 1)
            acc[plane, pl.ds(r, extent), :] += jnp.where(lane >= c, rolled, 0.0)
            acc[plane + 1, pl.ds(r, extent), :] += jnp.where(lane >= c, 0.0, rolled)

    def steps(slots):
        n = range(len(slots))
        field = [[probe[2 * m], probe[2 * m + 1]] for m in modes]
        objects = [window(slot) for slot in slots]
        state = right([[times(field[m], objects[i][0]) for m in modes] for i in n], 1, 0)
        yield
        entering = left(state, 1, 0)
        yield
        state = right([[times(entering[i][m], objects[i][1]) for m in modes] for i in n], 0, 0)
        yield
        state = left(state, 0, 0)
        yield
        weight = [2.0 * (sum(state[i][m][c] * state[i][m][c] for m in modes for c in range(2)) - patterns_ref[slots[i]])
                  for i in n]
        state = right([[[weight[i] * state[i][m][c] for c in range(2)] for m in modes] for i in n], 0, 1)
        yield
        state = left(state, 0, 1)
        yield
        for i in n:
            grad = conj_times(entering[i][0], state[i][0])
            for m in modes[1:]:
                grad = add(grad, conj_times(entering[i][m], state[i][m]))
            deposit(slots[i], 1, grad)
        state = right([[conj_times(objects[i][1], state[i][m]) for m in modes] for i in n], 1, 1)
        yield
        state = left(state, 1, 1)
        yield
        for i in n:
            grad = conj_times(field[0], state[i][0])
            for m in modes[1:]:
                grad = add(grad, conj_times(field[m], state[i][m]))
            deposit(slots[i], 0, grad)
        for m in modes:
            term = conj_times(objects[0][0], state[0][m])
            for i in n[1:]:
                term = add(term, conj_times(objects[i][0], state[i][m]))
            probe_acc[2 * m] += term[0]
            probe_acc[2 * m + 1] += term[1]

    def run(*sets):
        running = [steps(slots) for slots in sets]
        while running:
            running = [r for r in running if next(r, "done") is None]

    count = scalars_ref[2 * most]
    fours = lax.shift_right_logical(count, 2)

    def four(j, carry):
        run([4 * j, 4 * j + 1], [4 * j + 2, 4 * j + 3])
        return carry

    lax.fori_loop(0, fours, four, 0)

    @pl.when(lax.bitwise_and(count, 2) == 2)
    def _():
        run([4 * fours], [4 * fours + 1])

    @pl.when(lax.bitwise_and(count, 1) == 1)
    def _():
        run([count - 1])

    for layer in range(SLICES):
        for half in range(HALVES):
            for part in range(2):
                target = (layer * HALVES + half) * 2 + part
                plane = (layer * 2 + part) * HALVES + half
                own_out[pl.ds(target, tile_rows, stride=8), :] = acc[plane, :tile_rows]
                next_out[pl.ds(target, extent, stride=8), :] = acc[plane, tile_rows:]
    for k in range(lanes):
        probe_out[pl.ds(k, extent, stride=lanes), :] = probe_acc[k]


def prepared(own, patterns):
    extent = patterns.shape[1]
    vmem = pl.BlockSpec(memory_space=pltpu.VMEM)
    parts = jnp.asarray(factors(extent))
    return pl.pallas_call(
        prepare,
        out_shape=(
            jax.ShapeDtypeStruct((8, own.shape[0] // 8, own.shape[1]), jnp.float32),
            jax.ShapeDtypeStruct(patterns.shape, jnp.float32),
            jax.ShapeDtypeStruct((8, 2 * extent, 2 * extent), jnp.bfloat16),
        ),
        in_specs=[pl.BlockSpec(memory_space=pltpu.HBM)] * 3,
        out_specs=(vmem,) * 3,
        scratch_shapes=[
            pltpu.VMEM(own.shape, jnp.float32),
            pltpu.VMEM(parts.shape, jnp.float32),
            pltpu.SemaphoreType.DMA((3,)),
        ],
        compiler_params=pltpu.CompilerParams(vmem_limit_bytes=16 * 1024 * 1024),
        cost_estimate=pl.CostEstimate(flops=0, bytes_accessed=6 * 1024 * 1024, transcendentals=0),
    )(own, patterns, parts)


def terms(scalars, planes, upper, probe, patterns, mats):
    extent = patterns.shape[1]
    rows = planes.shape[1] + extent
    smem = pl.BlockSpec(memory_space=pltpu.SMEM)
    vmem = pl.BlockSpec(memory_space=pltpu.VMEM)
    return pl.pallas_call(
        kernel,
        out_shape=(
            jax.ShapeDtypeStruct((planes.shape[1] * 8, extent), jnp.float32),
            jax.ShapeDtypeStruct(upper.shape, jnp.float32),
            jax.ShapeDtypeStruct(probe.shape, jnp.float32),
        ),
        in_specs=[smem] + [vmem] * 5,
        out_specs=(vmem,) * 3,
        scratch_shapes=[
            pltpu.VMEM((8, rows, extent), jnp.float32),
            pltpu.VMEM((8, rows, extent), jnp.float32),
            pltpu.VMEM((2 * MODES, extent, extent), jnp.float32),
            pltpu.VMEM((2 * MODES, extent, extent), jnp.float32),
        ],
        compiler_params=pltpu.CompilerParams(vmem_limit_bytes=40 * 1024 * 1024),
    )(scalars, planes, upper, probe, patterns, mats)


def flat(block):
    rows, k, parts, columns = block.shape
    split_up = block.reshape(rows, k, parts, columns // 128, 128)
    return split_up.transpose(0, 1, 3, 2, 4).reshape(-1, 128)


def unflat(value, shape):
    rows, k, parts, columns = shape
    return value.reshape(rows, k, columns // 128, parts, 128).transpose(0, 1, 3, 2, 4).reshape(shape)


def shards(object_slices, probe_field, patterns, row_offsets, col_offsets, counts):
    size = lax.axis_size("tile")
    groups = [list(range(g, g + GROUP_DEV)) for g in range(0, size, GROUP_DEV)]
    own = flat(object_slices)
    mine = flat(probe_field)
    copies = jnp.broadcast_to(mine[None], (GROUP_DEV,) + mine.shape)
    probe = lax.all_to_all(copies, "tile", 0, 0, axis_index_groups=groups).reshape(-1, mine.shape[1])
    upper = lax.ppermute(own, "tile", [((i + 1) % size, i) for i in range(size)])
    own, patterns, probe = lax.optimization_barrier((own, patterns, probe))
    planes, patterns, mats = prepared(own, patterns)
    scalars = jnp.concatenate([row_offsets, col_offsets, counts])
    own_grad, upper_grad, probe_grad = terms(scalars, planes, upper, probe, patterns, mats)
    back = lax.ppermute(upper_grad, "tile", [(i, (i + 1) % size) for i in range(size)])
    blocks = lax.all_to_all(probe_grad.reshape(copies.shape), "tile", 0, 0, axis_index_groups=groups)
    return unflat(own_grad + back, object_slices.shape), unflat(jnp.sum(blocks, axis=0), probe_field.shape)


def solution(mesh):
    in_specs = (
        P(("groups", "tile"), None, None, None),
        P(("groups", "tile"), None, None, None),
        P(("groups", "tile"), None, None),
        P(("groups", "tile")),
        P(("groups", "tile")),
        P(("groups", "tile")),
    )
    out_specs = (P(("groups", "tile"), None, None, None), P(("groups", "tile"), None, None, None))
    return jax.shard_map(shards, mesh=mesh, in_specs=in_specs, out_specs=out_specs, check_vma=False)
```

time: 65.6 us -> 56.1 us (0.86); the launches traced: 66.8 us -> 56.5 us
  blocking collectives: 0 us -> 24.2 us
  starting transfers between devices: 29.7 us -> 13.3 us
  Pallas kernels: 14.1 us -> 4.21 us
  waiting for transfers between devices: 15.2 us -> 9.23 us
  local copies, waits for them, and re-layouts: 4.89 us -> 2.69 us
    ppermute x10 -> x0, starting transfers between devices: 26.2 us -> none  [partner(): lax.ppermute(value, 'tile', [(i, i ^ bits) for i in range(lax.axis_size('...]
    all_to_all x0 -> x1, blocking collectives: none -> 24.2 us  [shards(): lax.all_to_all(probe_grad.reshape(copies.shape), 'tile', 0, 0, axis_index...]
    ppermute x10 -> x0, waiting for transfers between devices: 15.2 us -> none  [partner(): lax.ppermute(value, 'tile', [(i, i ^ bits) for i in range(lax.axis_size('...]
    pallas_call x1, Pallas kernels: 13.9 us -> 3.82 us  [terms(): pl.pallas_call(kernel, out_shape=(jax.ShapeDtypeStruct((planes.shape[1] *...]
    all_to_all x0 -> x1, waiting for transfers between devices: none -> 9.22 us  [shards(): lax.all_to_all(copies, 'tile', 0, 0, axis_index_groups=groups)]
    ppermute x1, starting transfers between devices: 0.2 us -> 4.15 us  [shards(): lax.ppermute(upper_grad, 'tile', [(i, (i + 1) % size) for i in range(size)])]
    all_to_all x0 -> x1, starting transfers between devices: none -> 3.66 us  [shards(): lax.all_to_all(copies, 'tile', 0, 0, axis_index_groups=groups)]
    unnamed x16 -> x10, local copies, waits for them, and re-layouts: 4.87 us -> 1.25 us
  transfers between devices with their start and end apart: 12 -> 3, of which waited for: 6 -> 1; matrix products, arithmetic and copies ran while one was open for 2% -> 4% of each run, Pallas kernels for 0% -> 1%
where the time goes in v3:
time: 56.1 us; the launch traced here: 56.5 us
  blocking collectives  24.2 us (43%)
  starting transfers between devices  13.3 us (24%)
  waiting for transfers between devices  9.23 us (16%)
  Pallas kernels  4.21 us (8%)
  local copies, waits for them, and re-layouts  2.69 us (5%)
  other arithmetic  1.55 us (3%)
  between operations  1.37 us (2%)
    all_to_all x1, blocking collectives, shards(): lax.all_to_all(probe_grad.reshape(copies.shape), 'tile', 0, 0, axis_index...  24.2 us
    all_to_all x1, waiting for transfers between devices, shards(): lax.all_to_all(copies, 'tile', 0, 0, axis_index_groups=groups)  9.22 us
    ppermute x1, starting transfers between devices, shards(): lax.ppermute(own, 'tile', [((i + 1) % size, i) for i in range(size)])  5.47 us
    ppermute x1, starting transfers between devices, shards(): lax.ppermute(upper_grad, 'tile', [(i, (i + 1) % size) for i in range(size)])  4.15 us
    pallas_call x1, Pallas kernels, terms(): pl.pallas_call(kernel, out_shape=(jax.ShapeDtypeStruct((planes.shape[1] *...  3.82 us
    all_to_all x1, starting transfers between devices, shards(): lax.all_to_all(copies, 'tile', 0, 0, axis_index_groups=groups)  3.66 us
    broadcast_in_dim x1, local copies, waits for them, and re-layouts, shards(): copies = jnp.broadcast_to(mine[None], (GROUP_DEV,) + mine.shape)  1.44 us
    unnamed x10, local copies, waits for them, and re-layouts  1.25 us
  transfers between devices with their start and end apart: 3, of which 1 were waited for; matrix products, arithmetic and copies ran while one was open for 4% of the time, Pallas kernels for 1%

profile of v3, /device:TPU:0, one launch (start us, length us, event | category | flops | bytes accessed | tf_op | source)
XLA Modules:
  0.0 56.5 jit_solution(15965364980020136690)
XLA Ops:
  0.6 0.0 copy-start.1
  0.6 5.5 %collective-permute-start = (f32[1024,128]{1,0:T(8,128)}, f32[1024,128]{1,0:T(8,128)S(1)}, u32[]{:S(2)}, u32[]{:S(2)}) collective-permute-start(f32[1024,128]{1,0:T(8,128)} %bitcast.15), channel_id=1, source_target_pairs={{1,0},{2,1},{3,2},{4,3},{5,4},{6,5},{7,6},{8,7},{9,8},{10,9},{11,1... | collective-permute-start | bytes 1572872 | tf_op jit(solution)/shard_map/ppermute | solution.py:269
  6.1 1.4 %broadcast_in_dim.8 = f32[16,32,128]{2,1,0:T(8,128)} broadcast(f32[32,128]{1,0:T(8,128)} %bitcast.19), dimensions={1,2} | broadcast | bytes 278528 | tf_op jit(solution)/shard_map/broadcast_in_dim | solution.py:267
  7.6 0.0 copy-start.2
  7.6 3.7 %all-to-all-start = ((f32[16,32,128]{2,1,0:T(8,128)}), f32[16,32,128]{2,1,0:T(8,128)S(1)}, u32[]{:S(2)}, u32[]{:S(2)}) async-start(f32[16,32,128]{2,1,0:T(8,128)} %broadcast_in_dim.8), calls=%async_computation | async-start | bytes 524288 | tf_op jit(solution)/shard_map/all_to_all | solution.py:268
  11.2 0.0 copy-start.3
  11.2 0.0 copy-start.4
  11.9 0.0 copy-done.3
  11.9 0.0 copy-done.4
  11.9 0.1 pad_add_fusion.scalars_ref
  12.0 9.2 %all-to-all-done = f32[16,32,128]{2,1,0:T(8,128)S(1)} async-done(((f32[16,32,128]{2,1,0:T(8,128)}), f32[16,32,128]{2,1,0:T(8,128)S(1)}, u32[]{:S(2)}, u32[]{:S(2)}) %all-to-all-start) | async-done | bytes 262176 | tf_op jit(solution)/shard_map/all_to_all | solution.py:268
  21.2 0.0 copy-done.1
  21.2 0.0 copy-done.2
  21.2 0.0 copy-start
  21.2 1.2 %copy-done = f32[16,128,128]{2,1,0:T(8,128)S(1)} copy-done((f32[16,128,128]{2,1,0:T(8,128)S(1)}, f32[16,128,128]{2,1,0:T(8,128)}, u32[]{:S(2)}) %copy-start) | copy-done | bytes 1048600
  22.5 0.4 shard_map.86
  22.9 0.0 collective-permute-done.next_ref
  22.9 3.8 %shard_map.87 = (f32[1024,128]{1,0:T(8,128)S(1)}, f32[1024,128]{1,0:T(8,128)S(1)}, f32[512,128]{1,0:T(8,128)S(1)}) custom-call(s32[33]{0:T(128)S(1)} %pad_add_fusion.scalars_ref, f32[8,128,128]{2,1,0:T(8,128)S(1)} %get-tuple-element.13.own_ref, f32[1024,128]{1,0:T(8,128)S(1)} %collective-permute-done.next_ref, f32[512,128]{1,0:T(8,128)S(1)} %bitcast.14, ...), custom_call_target="tpu_custom_call" | custom-call | tf_op jit(solution)/shard_map/pallas_call | solution.py:232
  26.7 4.2 %collective-permute-start.1 = (f32[1024,128]{1,0:T(8,128)S(1)}, f32[1024,128]{1,0:T(8,128)S(1)}, u32[]{:S(2)}, u32[]{:S(2)}) collective-permute-start(f32[1024,128]{1,0:T(8,128)S(1)} %get-tuple-element.18), channel_id=1, source_target_pairs={{0,1},{1,2},{2,3},{3,4},{4,5},{5,6},{6,7},{7,8},{8,9},{9,10},{10,1... | collective-permute-start | bytes 1572872 | tf_op jit(solution)/shard_map/ppermute | solution.py:274
  30.9 24.2 %all_to_all.10 = f32[16,32,128]{2,1,0:T(8,128)S(1)} all-to-all(f32[16,32,128]{2,1,0:T(8,128)S(1)} %bitcast.17), channel_id=1, replica_groups={{0,1,2,3,4,5,6,7,8,9,10,11,12,13,14,15},{16,17,18,19,20,21,22,23,24,25,..., dimensions={0} | all-to-all | bytes 524288 | tf_op jit(solution)/shard_map/all_to_all | solution.py:275
  55.1 0.6 %reduce_sum.9 = f32[32,128]{1,0:T(8,128)} reduce(f32[16,32,128]{2,1,0:T(8,128)S(1)} %all_to_all.10, f32[]{:T(128)} %constant.1.clone.1), dimensions={0}, to_apply=%region_0.0 | reduce | flops 61440 | bytes 278532 | tf_op jit(solution)/shard_map/reduce_sum | solution.py:276
  55.7 0.0 collective-permute-done.1
  55.7 0.8 %add.3 = f32[1024,128]{1,0:T(8,128)} add(f32[1024,128]{1,0:T(8,128)S(1)} %get-tuple-element.17, f32[1024,128]{1,0:T(8,128)S(1)} %collective-permute-done.1) | non-fusion elementwise | flops 131072 | bytes 1572864 | tf_op jit(solution)/shard_map/add | solution.py:276
Async XLA Ops:
  0.6 20.6 %copy-start.1 = (f32[128,2,2,256]{3,2,1,0:T(2,128)S(1)}, f32[128,2,2,256]{3,2,1,0:T(2,128)}, u32[]{:S(2)}) copy-start(f32[128,2,2,256]{3,2,1,0:T(2,128)} %param.7) | copy-start | bytes 1572868
  0.6 22.2 %collective-permute-start = (f32[1024,128]{1,0:T(8,128)}, f32[1024,128]{1,0:T(8,128)S(1)}, u32[]{:S(2)}, u32[]{:S(2)}) collective-permute-start(f32[1024,128]{1,0:T(8,128)} %bitcast.15), channel_id=1, source_target_pairs={{1,0},{2,1},{3,2},{4,3},{5,4},{6,5},{7,6},{8,7},{9,8},{10,9},{11,1... | collective-permute-start | bytes 1572872 | tf_op jit(solution)/shard_map/ppermute | solution.py:269
  7.6 13.7 %copy-start.2 = (f32[4,128,128]{2,1,0:T(8,128)S(1)}, f32[4,128,128]{2,1,0:T(8,128)}, u32[]{:S(2)}) copy-start(f32[4,128,128]{2,1,0:T(8,128)} %constant.4.clone.factors_ref) | copy-start | bytes 786436
  7.6 13.7 %all-to-all-start = ((f32[16,32,128]{2,1,0:T(8,128)}), f32[16,32,128]{2,1,0:T(8,128)S(1)}, u32[]{:S(2)}, u32[]{:S(2)}) async-start(f32[16,32,128]{2,1,0:T(8,128)} %broadcast_in_dim.8), calls=%async_computation | async-start | bytes 524288 | tf_op jit(solution)/shard_map/all_to_all | solution.py:268
  11.2 0.7 %copy-start.3 = (s32[16]{0:T(128)S(1)}, s32[16]{0:T(128)}, u32[]{:S(2)}) copy-start(s32[16]{0:T(128)} %param.11) | copy-start | bytes 196
  11.2 0.7 %copy-start.4 = (s32[16]{0:T(128)S(1)}, s32[16]{0:T(128)}, u32[]{:S(2)}) copy-start(s32[16]{0:T(128)} %param.10) | copy-start | bytes 196
  21.2 1.2 %copy-start = (f32[16,128,128]{2,1,0:T(8,128)S(1)}, f32[16,128,128]{2,1,0:T(8,128)}, u32[]{:S(2)}) copy-start(f32[16,128,128]{2,1,0:T(8,128)} %patterns_ref) | copy-start | bytes 3145732
  26.7 29.0 %collective-permute-start.1 = (f32[1024,128]{1,0:T(8,128)S(1)}, f32[1024,128]{1,0:T(8,128)S(1)}, u32[]{:S(2)}, u32[]{:S(2)}) collective-permute-start(f32[1024,128]{1,0:T(8,128)S(1)} %get-tuple-element.18), channel_id=1, source_target_pairs={{0,1},{1,2},{2,3},{3,4},{4,5},{5,6},{6,7},{7,8},{8,9},{9,10},{10,1... | collective-permute-start | bytes 1572872 | tf_op jit(solution)/shard_map/ppermute | solution.py:274

commit v4 on v3

--- a/solution.py
+++ b/solution.py
@@ -13,6 +13,8 @@
 MODES = 2
 SLICES = 2
 HALVES = 2
+AHEAD = (0, 8, 4, 12, 2, 10, 6, 14)
+BACK = (0, 2, 8, 10, 4, 6, 12, 14)
 
 
 def factors(extent):
@@ -69,9 +71,26 @@
     return [a[0] + b[0], a[1] + b[1]]
 
 
-def kernel(scalars_ref, own_ref, next_ref, probe_ref, patterns_ref, mats_ref,
-           own_out, next_out, probe_out, obj, acc, probe, probe_acc):
+def member_rows(member, order, share):
+    return pl.ds(pl.multiple_of(lax.bitwise_xor(member, order) * share, share), share)
+
+
+def place(probe_ref, keep_out, send_out):
+    lanes, extent = probe_ref.shape[:2]
+    share = extent // GROUP_DEV
+    member = lax.rem(lax.axis_index("tile"), GROUP_DEV)
+    for odd, ref in enumerate((keep_out, send_out)):
+        for block, order in enumerate(BACK):
+            for k in range(lanes):
+                rows = pl.ds(block * share * lanes + k, share, stride=lanes)
+                ref[rows, :] = probe_ref[k, member_rows(member, order + odd, share), :]
+
+
+def kernel(scalars_ref, own_ref, next_ref, near_ref, far_ref, patterns_ref, mats_ref,
+           own_out, next_out, probe_acc, obj, acc, probe):
     most, extent = patterns_ref.shape[:2]
+    share = extent // GROUP_DEV
+    member = lax.rem(lax.axis_index("tile"), GROUP_DEV)
     tile_rows = own_ref.shape[1]
     lanes = 2 * MODES
     modes = range(MODES)
@@ -83,8 +102,11 @@
                 plane = (layer * 2 + part) * HALVES + half
                 obj[plane, :tile_rows] = own_ref[plane]
                 obj[plane, tile_rows:] = next_ref[pl.ds(source, extent, stride=8), :]
-    for k in range(lanes):
-        probe[k] = probe_ref[pl.ds(k, extent, stride=lanes), :]
+    for odd, ref in enumerate((near_ref, far_ref)):
+        for block, order in enumerate(AHEAD):
+            for k in range(lanes):
+                rows = pl.ds(block * share * lanes + k, share, stride=lanes)
+                probe[k, member_rows(member, order + odd, share), :] = ref[rows, :]
     acc[...] = jnp.zeros(acc.shape, jnp.float32)
     probe_acc[...] = jnp.zeros(probe_acc.shape, jnp.float32)
 
@@ -197,8 +219,6 @@
                 plane = (layer * 2 + part) * HALVES + half
                 own_out[pl.ds(target, tile_rows, stride=8), :] = acc[plane, :tile_rows]
                 next_out[pl.ds(target, extent, stride=8), :] = acc[plane, tile_rows:]
-    for k in range(lanes):
-        probe_out[pl.ds(k, extent, stride=lanes), :] = probe_acc[k]
 
 
 def prepared(own, patterns):
@@ -224,7 +244,7 @@
     )(own, patterns, parts)
 
 
-def terms(scalars, planes, upper, probe, patterns, mats):
+def terms(scalars, planes, upper, near, far, patterns, mats):
     extent = patterns.shape[1]
     rows = planes.shape[1] + extent
     smem = pl.BlockSpec(memory_space=pltpu.SMEM)
@@ -234,18 +254,28 @@
         out_shape=(
             jax.ShapeDtypeStruct((planes.shape[1] * 8, extent), jnp.float32),
             jax.ShapeDtypeStruct(upper.shape, jnp.float32),
-            jax.ShapeDtypeStruct(probe.shape, jnp.float32),
+            jax.ShapeDtypeStruct((2 * MODES, extent, extent), jnp.float32),
         ),
-        in_specs=[smem] + [vmem] * 5,
+        in_specs=[smem] + [vmem] * 6,
         out_specs=(vmem,) * 3,
         scratch_shapes=[
             pltpu.VMEM((8, rows, extent), jnp.float32),
             pltpu.VMEM((8, rows, extent), jnp.float32),
             pltpu.VMEM((2 * MODES, extent, extent), jnp.float32),
-            pltpu.VMEM((2 * MODES, extent, extent), jnp.float32),
         ],
         compiler_params=pltpu.CompilerParams(vmem_limit_bytes=40 * 1024 * 1024),
-    )(scalars, planes, upper, probe, patterns, mats)
+    )(scalars, planes, upper, near, far, patterns, mats)
+
+
+def placed(probe_grad, shape):
+    vmem = pl.BlockSpec(memory_space=pltpu.VMEM)
+    return pl.pallas_call(
+        place,
+        out_shape=(jax.ShapeDtypeStruct(shape, jnp.float32),) * 2,
+        in_specs=[vmem],
+        out_specs=(vmem,) * 2,
+        compiler_params=pltpu.CompilerParams(vmem_limit_bytes=4 * 1024 * 1024),
+    )(probe_grad)
 
 
 def flat(block):
@@ -259,21 +289,43 @@
     return value.reshape(rows, k, columns // 128, parts, 128).transpose(0, 1, 3, 2, 4).reshape(shape)
 
 
+def partner(value, bits):
+    return lax.ppermute(value, "tile", [(i, i ^ bits) for i in range(lax.axis_size("tile"))])
+
+
+def halved(value):
+    return value[:value.shape[0] // 2], value[value.shape[0] // 2:]
+
+
 def shards(object_slices, probe_field, patterns, row_offsets, col_offsets, counts):
     size = lax.axis_size("tile")
-    groups = [list(range(g, g + GROUP_DEV)) for g in range(0, size, GROUP_DEV)]
     own = flat(object_slices)
-    mine = flat(probe_field)
-    copies = jnp.broadcast_to(mine[None], (GROUP_DEV,) + mine.shape)
-    probe = lax.all_to_all(copies, "tile", 0, 0, axis_index_groups=groups).reshape(-1, mine.shape[1])
+    scalars = jnp.concatenate([row_offsets, col_offsets, counts])
+
     upper = lax.ppermute(own, "tile", [((i + 1) % size, i) for i in range(size)])
-    own, patterns, probe = lax.optimization_barrier((own, patterns, probe))
+    near = flat(probe_field)
+    for bits in (8, 4):
+        near = jnp.concatenate([near, partner(near, bits)], axis=0)
+    near, patterns, own = lax.optimization_barrier((near, patterns, own))
+    near = jnp.concatenate([near, partner(near, 2)], axis=0)
     planes, patterns, mats = prepared(own, patterns)
-    scalars = jnp.concatenate([row_offsets, col_offsets, counts])
-    own_grad, upper_grad, probe_grad = terms(scalars, planes, upper, probe, patterns, mats)
-    back = lax.ppermute(upper_grad, "tile", [(i, (i + 1) % size) for i in range(size)])
-    blocks = lax.all_to_all(probe_grad.reshape(copies.shape), "tile", 0, 0, axis_index_groups=groups)
-    return unflat(own_grad + back, object_slices.shape), unflat(jnp.sum(blocks, axis=0), probe_field.shape)
+    near, planes, patterns, mats, scalars = lax.optimization_barrier((near, planes, patterns, mats, scalars))
+    far = partner(near, 1)
+
+    own_grad, back, probe_grad = terms(scalars, planes, upper, near, far, patterns, mats)
+
+    back = lax.ppermute(back, "tile", [(i, (i + 1) % size) for i in range(size)])
+    keep, send = placed(probe_grad, near.shape)
+    total = keep + partner(send, 1)
+    for bits in (4, 8):
+        keep, send = halved(total)
+        total = keep + partner(send, bits)
+    back, total = lax.optimization_barrier((back, total))
+    keep, send = halved(total)
+    send = partner(send, 2)
+    object_grad = own_grad + back
+    object_grad, send = lax.optimization_barrier((object_grad, send))
+    return unflat(object_grad, object_slices.shape), unflat(keep + send, probe_field.shape)
 
 
 def solution(mesh):

time: 56.1 us -> 58.1 us (1.036); the launches traced: 56.5 us -> 57.6 us
  blocking collectives: 24.2 us -> 0 us
  waiting for transfers between devices: 9.23 us -> 22.4 us
  starting transfers between devices: 13.3 us -> 23.5 us
  other arithmetic: 1.55 us -> 2.3 us
    all_to_all x1 -> x0, blocking collectives: 24.2 us -> none  [shards(): lax.all_to_all(probe_grad.reshape(copies.shape), 'tile', 0, 0, axis_index...]
    ppermute x1 -> x9, waiting for transfers between devices: 0.01 us -> 22.4 us  [the longest x8 18.7 us: partner(): lax.ppermute(value, 'tile', [(i, i ^ bits) for i in range(lax.axis_size('...]
    ppermute x1 -> x9, starting transfers between devices: 4.15 us -> 22.1 us  [the longest x8 22 us: partner(): lax.ppermute(value, 'tile', [(i, i ^ bits) for i in range(lax.axis_size('...]
    all_to_all x1 -> x0, waiting for transfers between devices: 9.22 us -> none  [shards(): lax.all_to_all(copies, 'tile', 0, 0, axis_index_groups=groups)]
    ppermute x1, starting transfers between devices: 5.47 us -> 1.45 us  [shards(): lax.ppermute(own, 'tile', [((i + 1) % size, i) for i in range(size)])]
    all_to_all x1 -> x0, starting transfers between devices: 3.66 us -> none  [shards(): lax.all_to_all(copies, 'tile', 0, 0, axis_index_groups=groups)]
    unnamed x10 -> x12, local copies, waits for them, and re-layouts: 1.25 us -> 3.23 us
    broadcast_in_dim x1 -> x0, local copies, waits for them, and re-layouts: 1.44 us -> none  [shards(): copies = jnp.broadcast_to(mine[None], (GROUP_DEV,) + mine.shape)]
  transfers between devices with their start and end apart: 3 -> 10, of which waited for: 1 -> 9; matrix products, arithmetic and copies ran while one was open for 4% -> 3% of each run, Pallas kernels for 1% -> 1%
where the time goes in v4:
time: 58.1 us; the launch traced here: 57.6 us
  starting transfers between devices  23.5 us (40%)
  waiting for transfers between devices  22.4 us (39%)
  Pallas kernels  4.7 us (8%)
  local copies, waits for them, and re-layouts  3.25 us (6%)
  other arithmetic  2.3 us (4%)
  between operations  1.4 us (2%)
    ppermute x8, starting transfers between devices, partner(): lax.ppermute(value, 'tile', [(i, i ^ bits) for i in range(lax.axis_size('...  22 us
    ppermute x8, waiting for transfers between devices, partner(): lax.ppermute(value, 'tile', [(i, i ^ bits) for i in range(lax.axis_size('...  18.7 us
    pallas_call x1, Pallas kernels, terms(): pl.pallas_call(kernel, out_shape=(jax.ShapeDtypeStruct((planes.shape[1] *...  4.27 us
    ppermute x1, waiting for transfers between devices, shards(): lax.ppermute(back, 'tile', [(i, (i + 1) % size) for i in range(size)])  3.79 us
    unnamed x12, local copies, waits for them, and re-layouts  3.23 us
    ppermute x1, starting transfers between devices, shards(): lax.ppermute(own, 'tile', [((i + 1) % size, i) for i in range(size)])  1.45 us
  transfers between devices with their start and end apart: 10, of which 9 were waited for; matrix products, arithmetic and copies ran while one was open for 3% of the time, Pallas kernels for 1%

profile of v4, /device:TPU:0, one launch (start us, length us, event | category | flops | bytes accessed | tf_op | source)
XLA Modules:
  0.0 57.6 jit_solution(6064176015174176396)
XLA Ops:
  0.6 4.1 %collective-permute-start = (f32[32,128]{1,0:T(8,128)}, f32[32,128]{1,0:T(8,128)S(1)}, u32[]{:S(2)}, u32[]{:S(2)}) collective-permute-start(f32[32,128]{1,0:T(8,128)} %bitcast.15), channel_id=1, source_target_pairs={{0,8},{1,9},{2,10},{3,11},{4,12},{5,13},{6,14},{7,15},{8,0},{9,1},... | collective-permute-start | bytes 49160 | tf_op jit(solution)/shard_map/ppermute | solution.py:293
  4.7 0.0 copy-start.3
  4.7 1.5 %collective-permute-start.3 = (f32[1024,128]{1,0:T(8,128)}, f32[1024,128]{1,0:T(8,128)S(1)}, u32[]{:S(2)}, u32[]{:S(2)}) collective-permute-start(f32[1024,128]{1,0:T(8,128)} %bitcast.12), channel_id=1, source_target_pairs={{1,0},{2,1},{3,2},{4,3},{5,4},{6,5},{7,6},{8,7},{9,8},{10,9},{11,1... | collective-permute-start | bytes 1572872 | tf_op jit(solution)/shard_map/ppermute | solution.py:305
  6.2 0.5 collective-permute-done
  6.7 0.7 %pad_maximum_fusion.2 = f32[64,128]{1,0:T(8,128)S(1)} fusion(f32[32,128]{1,0:T(8,128)S(1)} %collective-permute-done, f32[32,128]{1,0:T(8,128)} %bitcast.16), kind=kLoop, calls=%fused_computation.4 | loop fusion | flops 8192 | bytes 65536 | tf_op jit(solution)/shard_map/concatenate | solution.py:308
  7.4 1.9 %collective-permute-start.1 = (f32[64,128]{1,0:T(8,128)S(1)}, f32[64,128]{1,0:T(8,128)S(1)}, u32[]{:S(2)}, u32[]{:S(2)}) collective-permute-start(f32[64,128]{1,0:T(8,128)S(1)} %pad_maximum_fusion.2), channel_id=1, source_target_pairs={{0,4},{1,5},{2,6},{3,7},{4,0},{5,1},{6,2},{7,3},{8,12},{9,13},{10,... | collective-permute-start | bytes 98312 | tf_op jit(solution)/shard_map/ppermute | solution.py:293
  9.9 0.0 copy-start.4
  10.0 0.0 copy-start.5
  10.0 5.0 %collective-permute-done.1 = f32[64,128]{1,0:T(8,128)S(1)} collective-permute-done((f32[64,128]{1,0:T(8,128)S(1)}, f32[64,128]{1,0:T(8,128)S(1)}, u32[]{:S(2)}, u32[]{:S(2)}) %collective-permute-start.1) | collective-permute-done | bytes 32800 | tf_op jit(solution)/shard_map/ppermute | solution.py:293
  15.0 0.0 copy-done.3
  15.0 0.1 collective-permute-start.2
  15.0 0.0 copy-done.4
  15.1 0.0 copy-done.5
  15.1 0.1 pad_add_fusion.scalars_ref
  15.1 0.0 copy-start
  15.1 1.2 %copy-done = f32[16,128,128]{2,1,0:T(8,128)S(1)} copy-done((f32[16,128,128]{2,1,0:T(8,128)S(1)}, f32[16,128,128]{2,1,0:T(8,128)}, u32[]{:S(2)}) %copy-start) | copy-done | bytes 1048600
  16.4 0.0 copy-start.1
  16.4 1.0 %copy-done.1 = f32[128,2,2,256]{3,2,1,0:T(2,128)S(1)} copy-done((f32[128,2,2,256]{3,2,1,0:T(2,128)S(1)}, f32[128,2,2,256]{3,2,1,0:T(2,128)}, u32[]{:S(2)}) %copy-start.1) | copy-done | bytes 524312
  17.4 0.0 copy-start.2
  17.4 0.9 %copy-done.2 = f32[4,128,128]{2,1,0:T(8,128)S(1)} copy-done((f32[4,128,128]{2,1,0:T(8,128)S(1)}, f32[4,128,128]{2,1,0:T(8,128)}, u32[]{:S(2)}) %copy-start.2) | copy-done | bytes 262168
  18.4 0.4 shard_map.86
  18.8 0.5 collective-permute-done.2
  19.3 0.1 collective-permute-start.4
  19.4 1.3 %collective-permute-done.4.far_ref = f32[256,128]{1,0:T(8,128)S(1)} collective-permute-done((f32[256,128]{1,0:T(8,128)S(1)}, f32[256,128]{1,0:T(8,128)S(1)}, u32[]{:S(2)}, u32[]{:S(2)}) %collective-permute-start.4) | collective-permute-done | bytes 131104 | tf_op jit(solution)/shard_map/ppermute | solution.py:293
  20.7 0.0 collective-permute-done.3.next_ref
  20.7 4.3 %shard_map.87 = (f32[1024,128]{1,0:T(8,128)S(1)}, f32[1024,128]{1,0:T(8,128)S(1)}, f32[4,128,128]{2,1,0:T(8,128)S(1)}) custom-call(s32[33]{0:T(128)S(1)} %pad_add_fusion.scalars_ref, f32[8,128,128]{2,1,0:T(8,128)S(1)} %get-tuple-element.29.own_ref, f32[1024,128]{1,0:T(8,128)S(1)} %collective-permute-done.3.next_ref, ...), custom_call_target="tpu_custom_call" | custom-call | tf_op jit(solution)/shard_map/pallas_call | solution.py:252
  25.1 1.3 %collective-permute-start.6 = (f32[256,128]{1,0:T(8,128)S(1)}, f32[256,128]{1,0:T(8,128)S(1)}, u32[]{:S(2)}, u32[]{:S(2)}) collective-permute-start(f32[256,128]{1,0:T(8,128)S(1)} %get-tuple-element.37), channel_id=1, source_target_pairs={{0,1},{1,0},{2,3},{3,2},{4,5},{5,4},{6,7},{7,6},{8,9},{9,8},{10,11... | collective-permute-start | bytes 393224 | tf_op jit(solution)/shard_map/ppermute | solution.py:293
  26.4 1.0 %collective-permute-done.6 = f32[256,128]{1,0:T(8,128)S(1)} collective-permute-done((f32[256,128]{1,0:T(8,128)S(1)}, f32[256,128]{1,0:T(8,128)S(1)}, u32[]{:S(2)}, u32[]{:S(2)}) %collective-permute-start.6) | collective-permute-done | bytes 131104 | tf_op jit(solution)/shard_map/ppermute | solution.py:293
  27.4 14.5 %collective-permute-start.7 = (f32[128,128]{1,0:T(8,128)S(1)}, f32[128,128]{1,0:T(8,128)S(1)}, u32[]{:S(2)}, u32[]{:S(2)}) collective-permute-start(f32[128,128]{1,0:T(8,128)S(1)} %slice.25), channel_id=1, source_target_pairs={{0,4},{1,5},{2,6},{3,7},{4,0},{5,1},{6,2},{7,3},{8,12},{9,13},{10,... | collective-permute-start | bytes 196616 | tf_op jit(solution)/shard_map/ppermute | solution.py:293
  41.9 0.1 collective-permute-start.5
  41.9 2.5 %collective-permute-done.7 = f32[128,128]{1,0:T(8,128)S(1)} collective-permute-done((f32[128,128]{1,0:T(8,128)S(1)}, f32[128,128]{1,0:T(8,128)S(1)}, u32[]{:S(2)}, u32[]{:S(2)}) %collective-permute-start.7) | collective-permute-done | bytes 65568 | tf_op jit(solution)/shard_map/ppermute | solution.py:293
  44.5 0.1 collective-permute-start.8
  44.6 4.9 %collective-permute-done.8 = f32[64,128]{1,0:T(8,128)S(1)} collective-permute-done((f32[64,128]{1,0:T(8,128)S(1)}, f32[64,128]{1,0:T(8,128)S(1)}, u32[]{:S(2)}, u32[]{:S(2)}) %collective-permute-start.8) | collective-permute-done | bytes 32800 | tf_op jit(solution)/shard_map/ppermute | solution.py:293
  49.5 3.8 %collective-permute-done.5 = f32[1024,128]{1,0:T(8,128)S(1)} collective-permute-done((f32[1024,128]{1,0:T(8,128)S(1)}, f32[1024,128]{1,0:T(8,128)S(1)}, u32[]{:S(2)}, u32[]{:S(2)}) %collective-permute-start.5) | collective-permute-done | bytes 524320 | tf_op jit(solution)/shard_map/ppermute | solution.py:317
  53.3 0.0 collective-permute-start.9
  53.3 0.8 %add.18 = f32[1024,128]{1,0:T(8,128)} add(f32[1024,128]{1,0:T(8,128)S(1)} %get-tuple-element.33, f32[1024,128]{1,0:T(8,128)S(1)} %collective-permute-done.5) | non-fusion elementwise | flops 131072 | bytes 1572864 | tf_op jit(solution)/shard_map/add | solution.py:326
  54.1 2.9 %collective-permute-done.9 = f32[32,128]{1,0:T(8,128)S(1)} collective-permute-done((f32[32,128]{1,0:T(8,128)S(1)}, f32[32,128]{1,0:T(8,128)S(1)}, u32[]{:S(2)}, u32[]{:S(2)}) %collective-permute-start.9) | collective-permute-done | bytes 16416 | tf_op jit(solution)/shard_map/ppermute | solution.py:293
  57.0 0.6 %slice_add_fusion.2 = f32[32,128]{1,0:T(8,128)} fusion(f32[32,128]{1,0:T(8,128)S(1)} %collective-permute-done.9, f32[64,128]{1,0:T(8,128)S(1)} %slice_add_fusion.1), kind=kLoop, calls=%fused_computation.5 | loop fusion | flops 4096 | bytes 49152 | tf_op jit(solution)/shard_map/add | solution.py:328
  (9 shorter events, 0.1 us)
Async XLA Ops:
  0.6 6.0 %collective-permute-start = (f32[32,128]{1,0:T(8,128)}, f32[32,128]{1,0:T(8,128)S(1)}, u32[]{:S(2)}, u32[]{:S(2)}) collective-permute-start(f32[32,128]{1,0:T(8,128)} %bitcast.15), channel_id=1, source_target_pairs={{0,8},{1,9},{2,10},{3,11},{4,12},{5,13},{6,14},{7,15},{8,0},{9,1},... | collective-permute-start | bytes 49160 | tf_op jit(solution)/shard_map/ppermute | solution.py:293
  4.7 10.2 %copy-start.3 = (f32[8,2,2,128]{3,2,1,0:T(2,128)S(1)}, f32[8,2,2,128]{3,2,1,0:T(2,128)}, u32[]{:S(2)}) copy-start(f32[8,2,2,128]{3,2,1,0:T(2,128)} %param.8) | copy-start | bytes 49156
  4.7 16.0 %collective-permute-start.3 = (f32[1024,128]{1,0:T(8,128)}, f32[1024,128]{1,0:T(8,128)S(1)}, u32[]{:S(2)}, u32[]{:S(2)}) collective-permute-start(f32[1024,128]{1,0:T(8,128)} %bitcast.12), channel_id=1, source_target_pairs={{1,0},{2,1},{3,2},{4,3},{5,4},{6,5},{7,6},{8,7},{9,8},{10,9},{11,1... | collective-permute-start | bytes 1572872 | tf_op jit(solution)/shard_map/ppermute | solution.py:305
  7.4 7.6 %collective-permute-start.1 = (f32[64,128]{1,0:T(8,128)S(1)}, f32[64,128]{1,0:T(8,128)S(1)}, u32[]{:S(2)}, u32[]{:S(2)}) collective-permute-start(f32[64,128]{1,0:T(8,128)S(1)} %pad_maximum_fusion.2), channel_id=1, source_target_pairs={{0,4},{1,5},{2,6},{3,7},{4,0},{5,1},{6,2},{7,3},{8,12},{9,13},{10,... | collective-permute-start | bytes 98312 | tf_op jit(solution)/shard_map/ppermute | solution.py:293
  9.9 5.1 %copy-start.4 = (s32[16]{0:T(128)S(1)}, s32[16]{0:T(128)}, u32[]{:S(2)}) copy-start(s32[16]{0:T(128)} %param.11) | copy-start | bytes 196
  10.0 5.1 %copy-start.5 = (s32[16]{0:T(128)S(1)}, s32[16]{0:T(128)}, u32[]{:S(2)}) copy-start(s32[16]{0:T(128)} %param.10) | copy-start | bytes 196
  15.0 4.3 %collective-permute-start.2 = (f32[128,128]{1,0:T(8,128)S(1)}, f32[128,128]{1,0:T(8,128)S(1)}, u32[]{:S(2)}, u32[]{:S(2)}) collective-permute-start(f32[128,128]{1,0:T(8,128)S(1)} %pad_maximum_fusion.1), channel_id=1, source_target_pairs={{0,2},{1,3},{2,0},{3,1},{4,6},{5,7},{6,4},{7,5},{8,10},{9,11},{10,... | collective-permute-start | bytes 196616 | tf_op jit(solution)/shard_map/ppermute | solution.py:293
  15.1 1.2 %copy-start = (f32[16,128,128]{2,1,0:T(8,128)S(1)}, f32[16,128,128]{2,1,0:T(8,128)}, u32[]{:S(2)}) copy-start(f32[16,128,128]{2,1,0:T(8,128)} %patterns_ref) | copy-start | bytes 3145732
  16.4 1.0 %copy-start.1 = (f32[128,2,2,256]{3,2,1,0:T(2,128)S(1)}, f32[128,2,2,256]{3,2,1,0:T(2,128)}, u32[]{:S(2)}) copy-start(f32[128,2,2,256]{3,2,1,0:T(2,128)} %param.7) | copy-start | bytes 1572868
  17.4 0.9 %copy-start.2 = (f32[4,128,128]{2,1,0:T(8,128)S(1)}, f32[4,128,128]{2,1,0:T(8,128)}, u32[]{:S(2)}) copy-start(f32[4,128,128]{2,1,0:T(8,128)} %constant.2.clone.factors_ref) | copy-start | bytes 786436
  19.3 1.4 %collective-permute-start.4 = (f32[256,128]{1,0:T(8,128)S(1)}, f32[256,128]{1,0:T(8,128)S(1)}, u32[]{:S(2)}, u32[]{:S(2)}) collective-permute-start(f32[256,128]{1,0:T(8,128)S(1)} %pad_maximum_fusion.near_ref), channel_id=1, source_target_pairs={{0,1},{1,0},{2,3},{3,2},{4,5},{5,4},{6,7},{7,6},{8,9},{9,8},{10,11... | collective-permute-start | bytes 393224 | tf_op jit(solution)/shard_map/ppermute | solution.py:293
  25.1 2.3 %collective-permute-start.6 = (f32[256,128]{1,0:T(8,128)S(1)}, f32[256,128]{1,0:T(8,128)S(1)}, u32[]{:S(2)}, u32[]{:S(2)}) collective-permute-start(f32[256,128]{1,0:T(8,128)S(1)} %get-tuple-element.37), channel_id=1, source_target_pairs={{0,1},{1,0},{2,3},{3,2},{4,5},{5,4},{6,7},{7,6},{8,9},{9,8},{10,11... | collective-permute-start | bytes 393224 | tf_op jit(solution)/shard_map/ppermute | solution.py:293
  27.4 17.1 %collective-permute-start.7 = (f32[128,128]{1,0:T(8,128)S(1)}, f32[128,128]{1,0:T(8,128)S(1)}, u32[]{:S(2)}, u32[]{:S(2)}) collective-permute-start(f32[128,128]{1,0:T(8,128)S(1)} %slice.25), channel_id=1, source_target_pairs={{0,4},{1,5},{2,6},{3,7},{4,0},{5,1},{6,2},{7,3},{8,12},{9,13},{10,... | collective-permute-start | bytes 196616 | tf_op jit(solution)/shard_map/ppermute | solution.py:293
  41.9 11.4 %collective-permute-start.5 = (f32[1024,128]{1,0:T(8,128)S(1)}, f32[1024,128]{1,0:T(8,128)S(1)}, u32[]{:S(2)}, u32[]{:S(2)}) collective-permute-start(f32[1024,128]{1,0:T(8,128)S(1)} %get-tuple-element.34), channel_id=1, source_target_pairs={{0,1},{1,2},{2,3},{3,4},{4,5},{5,6},{6,7},{7,8},{8,9},{9,10},{10,1... | collective-permute-start | bytes 1572872 | tf_op jit(solution)/shard_map/ppermute | solution.py:317
  44.5 5.0 %collective-permute-start.8 = (f32[64,128]{1,0:T(8,128)S(1)}, f32[64,128]{1,0:T(8,128)S(1)}, u32[]{:S(2)}, u32[]{:S(2)}) collective-permute-start(f32[64,128]{1,0:T(8,128)S(1)} %slice.27), channel_id=1, source_target_pairs={{0,8},{1,9},{2,10},{3,11},{4,12},{5,13},{6,14},{7,15},{8,0},{9,1},... | collective-permute-start | bytes 98312 | tf_op jit(solution)/shard_map/ppermute | solution.py:293
  53.3 3.7 %collective-permute-start.9 = (f32[32,128]{1,0:T(8,128)S(1)}, f32[32,128]{1,0:T(8,128)S(1)}, u32[]{:S(2)}, u32[]{:S(2)}) collective-permute-start(f32[32,128]{1,0:T(8,128)S(1)} %slice.22), channel_id=1, source_target_pairs={{0,2},{1,3},{2,0},{3,1},{4,6},{5,7},{6,4},{7,5},{8,10},{9,11},{10,... | collective-permute-start | bytes 49160 | tf_op jit(solution)/shard_map/ppermute | solution.py:293

commit v5 on v4

--- a/solution.py
+++ b/solution.py
@@ -13,8 +13,6 @@
 MODES = 2
 SLICES = 2
 HALVES = 2
-AHEAD = (0, 8, 4, 12, 2, 10, 6, 14)
-BACK = (0, 2, 8, 10, 4, 6, 12, 14)
 
 
 def factors(extent):
@@ -71,26 +69,25 @@
     return [a[0] + b[0], a[1] + b[1]]
 
 
-def member_rows(member, order, share):
-    return pl.ds(pl.multiple_of(lax.bitwise_xor(member, order) * share, share), share)
+def member_rows(number, odd, share):
+    core = lax.bitwise_xor(lax.rem(lax.axis_index("tile"), 2), odd)
+    return pl.ds(pl.multiple_of((2 * number + core) * share, share), share)
 
 
 def place(probe_ref, keep_out, send_out):
     lanes, extent = probe_ref.shape[:2]
     share = extent // GROUP_DEV
-    member = lax.rem(lax.axis_index("tile"), GROUP_DEV)
     for odd, ref in enumerate((keep_out, send_out)):
-        for block, order in enumerate(BACK):
+        for number in range(GROUP_DEV // 2):
             for k in range(lanes):
-                rows = pl.ds(block * share * lanes + k, share, stride=lanes)
-                ref[rows, :] = probe_ref[k, member_rows(member, order + odd, share), :]
+                rows = pl.ds(number * share * lanes + k, share, stride=lanes)
+                ref[rows, :] = probe_ref[k, member_rows(number, odd, share), :]
 
 
 def kernel(scalars_ref, own_ref, next_ref, near_ref, far_ref, patterns_ref, mats_ref,
            own_out, next_out, probe_acc, obj, acc, probe):
     most, extent = patterns_ref.shape[:2]
     share = extent // GROUP_DEV
-    member = lax.rem(lax.axis_index("tile"), GROUP_DEV)
     tile_rows = own_ref.shape[1]
     lanes = 2 * MODES
     modes = range(MODES)
@@ -103,10 +100,10 @@
                 obj[plane, :tile_rows] = own_ref[plane]
                 obj[plane, tile_rows:] = next_ref[pl.ds(source, extent, stride=8), :]
     for odd, ref in enumerate((near_ref, far_ref)):
-        for block, order in enumerate(AHEAD):
+        for number in range(GROUP_DEV // 2):
             for k in range(lanes):
-                rows = pl.ds(block * share * lanes + k, share, stride=lanes)
-                probe[k, member_rows(member, order + odd, share), :] = ref[rows, :]
+                rows = pl.ds(number * share * lanes + k, share, stride=lanes)
+                probe[k, member_rows(number, odd, share), :] = ref[rows, :]
     acc[...] = jnp.zeros(acc.shape, jnp.float32)
     probe_acc[...] = jnp.zeros(probe_acc.shape, jnp.float32)
 
@@ -289,43 +286,28 @@
     return value.reshape(rows, k, columns // 128, parts, 128).transpose(0, 1, 3, 2, 4).reshape(shape)
 
 
-def partner(value, bits):
-    return lax.ppermute(value, "tile", [(i, i ^ bits) for i in range(lax.axis_size("tile"))])
-
-
-def halved(value):
-    return value[:value.shape[0] // 2], value[value.shape[0] // 2:]
-
-
 def shards(object_slices, probe_field, patterns, row_offsets, col_offsets, counts):
     size = lax.axis_size("tile")
+    cores = [(i, i ^ 1) for i in range(size)]
+    alike = [list(range(g + core, g + GROUP_DEV, 2)) for g in range(0, size, GROUP_DEV) for core in range(2)]
     own = flat(object_slices)
+    mine = flat(probe_field)
     scalars = jnp.concatenate([row_offsets, col_offsets, counts])
 
     upper = lax.ppermute(own, "tile", [((i + 1) % size, i) for i in range(size)])
-    near = flat(probe_field)
-    for bits in (8, 4):
-        near = jnp.concatenate([near, partner(near, bits)], axis=0)
-    near, patterns, own = lax.optimization_barrier((near, patterns, own))
-    near = jnp.concatenate([near, partner(near, 2)], axis=0)
+    copies = jnp.broadcast_to(mine[None], (GROUP_DEV // 2,) + mine.shape)
+    near = lax.all_to_all(copies, "tile", 0, 0, axis_index_groups=alike).reshape(-1, mine.shape[1])
+    far = lax.ppermute(near, "tile", cores)
     planes, patterns, mats = prepared(own, patterns)
-    near, planes, patterns, mats, scalars = lax.optimization_barrier((near, planes, patterns, mats, scalars))
-    far = partner(near, 1)
 
     own_grad, back, probe_grad = terms(scalars, planes, upper, near, far, patterns, mats)
 
     back = lax.ppermute(back, "tile", [(i, (i + 1) % size) for i in range(size)])
     keep, send = placed(probe_grad, near.shape)
-    total = keep + partner(send, 1)
-    for bits in (4, 8):
-        keep, send = halved(total)
-        total = keep + partner(send, bits)
-    back, total = lax.optimization_barrier((back, total))
-    keep, send = halved(total)
-    send = partner(send, 2)
+    total = keep + lax.ppermute(send, "tile", cores)
+    blocks = lax.all_to_all(total.reshape(copies.shape), "tile", 0, 0, axis_index_groups=alike)
     object_grad = own_grad + back
-    object_grad, send = lax.optimization_barrier((object_grad, send))
-    return unflat(object_grad, object_slices.shape), unflat(keep + send, probe_field.shape)
+    return unflat(object_grad, object_slices.shape), unflat(jnp.sum(blocks, axis=0), probe_field.shape)
 
 
 def solution(mesh):

time: 58.1 us -> 54 us (0.929)
  the two profiles are of different devices: /device:TPU:0 before, /device:TPU:4 now
where the time goes in v5:
time: 54 us; the launch traced here: 53.3 us
  blocking collectives  29 us (54%)
  Pallas kernels  8.6 us (16%)
  starting transfers between devices  7.91 us (15%)
  local copies, waits for them, and re-layouts  3.27 us (6%)
  waiting for transfers between devices  1.62 us (3%)
  other arithmetic  1.55 us (3%)
  between operations  1.34 us (2%)
    all_to_all x1, blocking collectives, shards(): lax.all_to_all(total.reshape(copies.shape), 'tile', 0, 0, axis_index_grou...  19.3 us
    all_to_all x1, blocking collectives, shards(): lax.all_to_all(copies, 'tile', 0, 0, axis_index_groups=alike)  9.74 us
    pallas_call x1, Pallas kernels, terms(): pl.pallas_call(kernel, out_shape=(jax.ShapeDtypeStruct((planes.shape[1] *...  8.19 us
    ppermute x1, starting transfers between devices, shards(): lax.ppermute(own, 'tile', [((i + 1) % size, i) for i in range(size)])  4.02 us
    ppermute x1, starting transfers between devices, shards(): lax.ppermute(back, 'tile', [(i, (i + 1) % size) for i in range(size)])  3.79 us
    unnamed x10, local copies, waits for them, and re-layouts  2.54 us
    ppermute x1, waiting for transfers between devices, shards(): total = keep + lax.ppermute(send, 'tile', cores)  1.61 us
  transfers between devices with their start and end apart: 4, of which 1 were waited for; matrix products, arithmetic and copies ran while one was open for 3% of the time, Pallas kernels for 1%

profile of v5, /device:TPU:4, one launch (start us, length us, event | category | flops | bytes accessed | tf_op | source)
XLA Modules:
  0.0 53.3 jit_solution(5905926131363245086)
XLA Ops:
  0.6 0.0 copy-start.2
  0.6 4.0 %collective-permute-start = (f32[1024,128]{1,0:T(8,128)}, f32[1024,128]{1,0:T(8,128)S(1)}, u32[]{:S(2)}, u32[]{:S(2)}) collective-permute-start(f32[1024,128]{1,0:T(8,128)} %bitcast.14), channel_id=1, source_target_pairs={{1,0},{2,1},{3,2},{4,3},{5,4},{6,5},{7,6},{8,7},{9,8},{10,9},{11,1... | collective-permute-start | bytes 1572872 | tf_op jit(solution)/shard_map/ppermute | solution.py:297
  4.7 0.7 %broadcast_in_dim.8 = f32[8,32,128]{2,1,0:T(8,128)S(1)} broadcast(f32[32,128]{1,0:T(8,128)} %bitcast.20), dimensions={1,2} | broadcast | bytes 147456 | tf_op jit(solution)/shard_map/broadcast_in_dim | solution.py:298
  5.4 9.7 %all_to_all.10 = f32[8,32,128]{2,1,0:T(8,128)S(1)} all-to-all(f32[8,32,128]{2,1,0:T(8,128)S(1)} %broadcast_in_dim.8), channel_id=1, replica_groups={{0,2,4,6,8,10,12,14},{1,3,5,7,9,11,13,15},{16,18,20,22,24,26,28,30},{17..., dimensions={0} | all-to-all | bytes 262144 | tf_op jit(solution)/shard_map/all_to_all | solution.py:299
  15.1 0.0 collective-permute-start.1
  15.8 0.0 copy-done.2
  15.8 0.0 copy-start
  15.8 1.2 %copy-done = f32[16,128,128]{2,1,0:T(8,128)S(1)} copy-done((f32[16,128,128]{2,1,0:T(8,128)S(1)}, f32[16,128,128]{2,1,0:T(8,128)}, u32[]{:S(2)}) %copy-start) | copy-done | bytes 1048600
  17.0 0.0 copy-start.1
  17.0 1.0 %copy-done.1 = f32[128,2,2,256]{3,2,1,0:T(2,128)S(1)} copy-done((f32[128,2,2,256]{3,2,1,0:T(2,128)S(1)}, f32[128,2,2,256]{3,2,1,0:T(2,128)}, u32[]{:S(2)}) %copy-start.1) | copy-done | bytes 524312
  18.1 0.0 copy-start.3
  18.1 0.0 copy-start.4
  18.1 0.4 shard_map.86
  18.5 0.3 copy-done.3
  18.7 0.0 copy-done.4
  18.7 0.1 pad_add_fusion.scalars_ref
  18.8 0.0 collective-permute-done.1.far_ref
  18.8 0.0 collective-permute-done.next_ref
  18.8 8.2 %shard_map.87 = (f32[1024,128]{1,0:T(8,128)S(1)}, f32[1024,128]{1,0:T(8,128)S(1)}, f32[4,128,128]{2,1,0:T(8,128)S(1)}) custom-call(s32[33]{0:T(128)S(1)} %pad_add_fusion.scalars_ref, f32[8,128,128]{2,1,0:T(8,128)S(1)} %get-tuple-element.10.own_ref, f32[1024,128]{1,0:T(8,128)S(1)} %collective-permute-done.next_ref, f32[256,128]{1,0:T(8,128)S(1)} %bitcast.17, ...), custom_call_target="tpu_custom_call" | custom-call | tf_op jit(solution)/shard_map/pallas_call | solution.py:249
  27.0 3.8 %collective-permute-start.2 = (f32[1024,128]{1,0:T(8,128)S(1)}, f32[1024,128]{1,0:T(8,128)S(1)}, u32[]{:S(2)}, u32[]{:S(2)}) collective-permute-start(f32[1024,128]{1,0:T(8,128)S(1)} %get-tuple-element.14), channel_id=1, source_target_pairs={{0,1},{1,2},{2,3},{3,4},{4,5},{5,6},{6,7},{7,8},{8,9},{9,10},{10,1... | collective-permute-start | bytes 1572872 | tf_op jit(solution)/shard_map/ppermute | solution.py:305
  30.8 0.1 collective-permute-start.3
  30.9 1.6 %collective-permute-done.3 = f32[256,128]{1,0:T(8,128)S(1)} collective-permute-done((f32[256,128]{1,0:T(8,128)S(1)}, f32[256,128]{1,0:T(8,128)S(1)}, u32[]{:S(2)}, u32[]{:S(2)}) %collective-permute-start.3) | collective-permute-done | bytes 131104 | tf_op jit(solution)/shard_map/ppermute | solution.py:307
  32.5 19.3 %all_to_all.11 = f32[8,32,128]{2,1,0:T(8,128)S(1)} all-to-all(f32[8,32,128]{2,1,0:T(8,128)S(1)} %bitcast.19), channel_id=1, replica_groups={{0,2,4,6,8,10,12,14},{1,3,5,7,9,11,13,15},{16,18,20,22,24,26,28,30},{17..., dimensions={0} | all-to-all | bytes 262144 | tf_op jit(solution)/shard_map/all_to_all | solution.py:308
  51.8 0.6 %reduce_sum.9 = f32[32,128]{1,0:T(8,128)} reduce(f32[8,32,128]{2,1,0:T(8,128)S(1)} %all_to_all.11, f32[]{:T(128)} %constant.1.clone.1), dimensions={0}, to_apply=%region_0.0 | reduce | flops 28672 | bytes 147460 | tf_op jit(solution)/shard_map/reduce_sum | solution.py:310
  52.5 0.0 collective-permute-done.2
  52.5 0.8 %add.6 = f32[1024,128]{1,0:T(8,128)} add(f32[1024,128]{1,0:T(8,128)S(1)} %get-tuple-element.13, f32[1024,128]{1,0:T(8,128)S(1)} %collective-permute-done.2) | non-fusion elementwise | flops 131072 | bytes 1572864 | tf_op jit(solution)/shard_map/add | solution.py:309
  (2 shorter events, 0.0 us)
Async XLA Ops:
  0.6 15.2 %copy-start.2 = (f32[4,128,128]{2,1,0:T(8,128)S(1)}, f32[4,128,128]{2,1,0:T(8,128)}, u32[]{:S(2)}) copy-start(f32[4,128,128]{2,1,0:T(8,128)} %constant.4.clone.factors_ref) | copy-start | bytes 786436
  0.6 18.2 %collective-permute-start = (f32[1024,128]{1,0:T(8,128)}, f32[1024,128]{1,0:T(8,128)S(1)}, u32[]{:S(2)}, u32[]{:S(2)}) collective-permute-start(f32[1024,128]{1,0:T(8,128)} %bitcast.14), channel_id=1, source_target_pairs={{1,0},{2,1},{3,2},{4,3},{5,4},{6,5},{7,6},{8,7},{9,8},{10,9},{11,1... | collective-permute-start | bytes 1572872 | tf_op jit(solution)/shard_map/ppermute | solution.py:297
  15.1 3.7 %collective-permute-start.1 = (f32[256,128]{1,0:T(8,128)S(1)}, f32[256,128]{1,0:T(8,128)S(1)}, u32[]{:S(2)}, u32[]{:S(2)}) collective-permute-start(f32[256,128]{1,0:T(8,128)S(1)} %bitcast.16), channel_id=1, source_target_pairs={{0,1},{1,0},{2,3},{3,2},{4,5},{5,4},{6,7},{7,6},{8,9},{9,8},{10,11... | collective-permute-start | bytes 393224 | tf_op jit(solution)/shard_map/ppermute | solution.py:300
  15.8 1.2 %copy-start = (f32[16,128,128]{2,1,0:T(8,128)S(1)}, f32[16,128,128]{2,1,0:T(8,128)}, u32[]{:S(2)}) copy-start(f32[16,128,128]{2,1,0:T(8,128)} %patterns_ref.1) | copy-start | bytes 3145732
  17.0 1.0 %copy-start.1 = (f32[128,2,2,256]{3,2,1,0:T(2,128)S(1)}, f32[128,2,2,256]{3,2,1,0:T(2,128)}, u32[]{:S(2)}) copy-start(f32[128,2,2,256]{3,2,1,0:T(2,128)} %param.7) | copy-start | bytes 1572868
  18.1 0.7 %copy-start.3 = (s32[16]{0:T(128)S(1)}, s32[16]{0:T(128)}, u32[]{:S(2)}) copy-start(s32[16]{0:T(128)} %param.11) | copy-start | bytes 196
  18.1 0.7 %copy-start.4 = (s32[16]{0:T(128)S(1)}, s32[16]{0:T(128)}, u32[]{:S(2)}) copy-start(s32[16]{0:T(128)} %param.10) | copy-start | bytes 196
  27.0 25.4 %collective-permute-start.2 = (f32[1024,128]{1,0:T(8,128)S(1)}, f32[1024,128]{1,0:T(8,128)S(1)}, u32[]{:S(2)}, u32[]{:S(2)}) collective-permute-start(f32[1024,128]{1,0:T(8,128)S(1)} %get-tuple-element.14), channel_id=1, source_target_pairs={{0,1},{1,2},{2,3},{3,4},{4,5},{5,6},{6,7},{7,8},{8,9},{9,10},{10,1... | collective-permute-start | bytes 1572872 | tf_op jit(solution)/shard_map/ppermute | solution.py:305
  30.8 1.7 %collective-permute-start.3 = (f32[256,128]{1,0:T(8,128)S(1)}, f32[256,128]{1,0:T(8,128)S(1)}, u32[]{:S(2)}, u32[]{:S(2)}) collective-permute-start(f32[256,128]{1,0:T(8,128)S(1)} %get-tuple-element.17), channel_id=1, source_target_pairs={{0,1},{1,0},{2,3},{3,2},{4,5},{5,4},{6,7},{7,6},{8,9},{9,8},{10,11... | collective-permute-start | bytes 393224 | tf_op jit(solution)/shard_map/ppermute | solution.py:307

commit v6 on v4

--- a/solution.py
+++ b/solution.py
@@ -1,3 +1,4 @@
+import functools
 import math
 
 import jax
@@ -31,9 +32,9 @@
     return high, low
 
 
-def prepare(own_ref, patterns_ref, factors_ref, planes_out, patterns_out, mats_out, own, parts, sems):
+def prepare(own_ref, patterns_ref, factors_ref, own_out, patterns_out, mats_out, parts, sems):
     copies = [pltpu.make_async_copy(source, target, sems.at[i]) for i, (source, target) in enumerate(
-        ((factors_ref, parts), (own_ref, own), (patterns_ref, patterns_out)))]
+        ((factors_ref, parts), (own_ref, own_out), (patterns_ref, patterns_out)))]
     for copy in copies:
         copy.start()
     copies[0].wait()
@@ -49,13 +50,6 @@
                 mats_out[mat, extent:, :extent] = lower
                 mats_out[mat, extent:, extent:] = real[k]
     copies[1].wait()
-    rows = planes_out.shape[1]
-    for layer in range(SLICES):
-        for half in range(HALVES):
-            for part in range(2):
-                source = (layer * HALVES + half) * 2 + part
-                plane = (layer * 2 + part) * HALVES + half
-                planes_out[plane] = own[pl.ds(source, rows, stride=8), :]
     copies[2].wait()
 
 
@@ -86,29 +80,47 @@
                 ref[rows, :] = probe_ref[k, member_rows(member, order + odd, share), :]
 
 
-def kernel(scalars_ref, own_ref, next_ref, near_ref, far_ref, patterns_ref, mats_ref,
-           own_out, next_out, probe_acc, obj, acc, probe):
+def kernel(own_core, scalars_ref, paired_ref, own_ref, other_ref, above_own_ref, above_other_ref, near_ref, far_ref,
+           patterns_ref, odd_ref, mats_ref, start_ref, keep_out, send_out, probe_acc, obj, acc, probe):
     most, extent = patterns_ref.shape[:2]
     share = extent // GROUP_DEV
-    member = lax.rem(lax.axis_index("tile"), GROUP_DEV)
-    tile_rows = own_ref.shape[1]
+    place_in_tile = lax.axis_index("tile")
+    member = lax.rem(place_in_tile, GROUP_DEV)
+    is_own = lax.rem(place_in_tile, 2) == own_core
+    tile_rows = own_ref.shape[0] // 8
     lanes = 2 * MODES
     modes = range(MODES)
 
-    for layer in range(SLICES):
-        for half in range(HALVES):
-            for part in range(2):
-                source = (layer * HALVES + half) * 2 + part
-                plane = (layer * 2 + part) * HALVES + half
-                obj[plane, :tile_rows] = own_ref[plane]
-                obj[plane, tile_rows:] = next_ref[pl.ds(source, extent, stride=8), :]
+    def tiles(low, high, into):
+        for layer in range(SLICES):
+            for half in range(HALVES):
+                for part in range(2):
+                    source = (layer * HALVES + half) * 2 + part
+                    plane = (layer * 2 + part) * HALVES + half
+                    into(plane, slice(0, tile_rows), low, pl.ds(source, tile_rows, stride=8))
+                    into(plane, slice(tile_rows, tile_rows + extent), high, pl.ds(source, extent, stride=8))
+
+    def load(plane, rows, ref, strided):
+        obj[plane, rows] = ref[strided, :]
+
+    def store(plane, rows, ref, strided):
+        ref[strided, :] = acc[plane, rows]
+
+    @pl.when(is_own)
+    def _():
+        tiles(own_ref, above_own_ref, load)
+
+    @pl.when(jnp.logical_not(is_own))
+    def _():
+        tiles(other_ref, above_other_ref, load)
+
     for odd, ref in enumerate((near_ref, far_ref)):
         for block, order in enumerate(AHEAD):
             for k in range(lanes):
                 rows = pl.ds(block * share * lanes + k, share, stride=lanes)
                 probe[k, member_rows(member, order + odd, share), :] = ref[rows, :]
     acc[...] = jnp.zeros(acc.shape, jnp.float32)
-    probe_acc[...] = jnp.zeros(probe_acc.shape, jnp.float32)
+    probe_acc[...] = jnp.zeros(probe_acc.shape, jnp.float32) if start_ref is None else start_ref[...]
 
     def right(fields, kind, conj):
         high_m, low_m = mats_ref[4 * kind + 2 * conj], mats_ref[4 * kind + 2 * conj + 1]
@@ -130,8 +142,13 @@
 
     lane = lax.broadcasted_iota(jnp.int32, (extent, extent), 1)
 
+    def corner(slot):
+        own, odd = 2 * slot, 2 * slot + 1
+        return (jnp.where(is_own, scalars_ref[own], paired_ref[odd]),
+                jnp.where(is_own, scalars_ref[most + own], paired_ref[most + odd]))
+
     def window(slot):
-        r, c = scalars_ref[slot], scalars_ref[most + slot]
+        r, c = corner(slot)
         shift = lax.rem(extent - c, extent)
         layers = []
         for layer in range(SLICES):
@@ -144,7 +161,7 @@
         return layers
 
     def deposit(slot, layer, grad):
-        r, c = scalars_ref[slot], scalars_ref[most + slot]
+        r, c = corner(slot)
         for part in range(2):
             plane = (layer * 2 + part) * HALVES
             rolled = pltpu.roll(grad[part], lax.rem(c, extent), 1)
@@ -163,8 +180,11 @@
         yield
         state = left(state, 0, 0)
         yield
-        weight = [2.0 * (sum(state[i][m][c] * state[i][m][c] for m in modes for c in range(2)) - patterns_ref[slots[i]])
-                  for i in n]
+        weight = []
+        for i in n:
+            intensity = sum(state[i][m][c] * state[i][m][c] for m in modes for c in range(2))
+            measured = jnp.where(is_own, patterns_ref[2 * slots[i]], odd_ref[slots[i]])
+            weight.append(jnp.where(slots[i] < count, 2.0 * (intensity - measured), 0.0))
         state = right([[[weight[i] * state[i][m][c] for c in range(2)] for m in modes] for i in n], 0, 1)
         yield
         state = left(state, 0, 1)
@@ -195,8 +215,10 @@
         while running:
             running = [r for r in running if next(r, "done") is None]
 
-    count = scalars_ref[2 * most]
-    fours = lax.shift_right_logical(count, 2)
+    count = jnp.where(is_own, lax.shift_right_logical(scalars_ref[2 * most] + 1, 1),
+                      lax.shift_right_logical(paired_ref[2 * most], 1))
+    fours = lax.shift_right_logical(count + 1, 2)
+    left_over = count - 4 * fours
 
     def four(j, carry):
         run([4 * j, 4 * j + 1], [4 * j + 2, 4 * j + 3])
@@ -204,21 +226,21 @@
 
     lax.fori_loop(0, fours, four, 0)
 
-    @pl.when(lax.bitwise_and(count, 2) == 2)
+    @pl.when(left_over == 2)
     def _():
         run([4 * fours], [4 * fours + 1])
 
-    @pl.when(lax.bitwise_and(count, 1) == 1)
-    def _():
-        run([count - 1])
-
-    for layer in range(SLICES):
-        for half in range(HALVES):
-            for part in range(2):
-                target = (layer * HALVES + half) * 2 + part
-                plane = (layer * 2 + part) * HALVES + half
-                own_out[pl.ds(target, tile_rows, stride=8), :] = acc[plane, :tile_rows]
-                next_out[pl.ds(target, extent, stride=8), :] = acc[plane, tile_rows:]
+    @pl.when(left_over == 1)
+    def _():
+        run([4 * fours])
+
+    @pl.when(is_own)
+    def _():
+        tiles(keep_out, send_out, store)
+
+    @pl.when(jnp.logical_not(is_own))
+    def _():
+        tiles(send_out, keep_out, store)
 
 
 def prepared(own, patterns):
@@ -228,43 +250,47 @@
     return pl.pallas_call(
         prepare,
         out_shape=(
-            jax.ShapeDtypeStruct((8, own.shape[0] // 8, own.shape[1]), jnp.float32),
+            jax.ShapeDtypeStruct(own.shape, jnp.float32),
             jax.ShapeDtypeStruct(patterns.shape, jnp.float32),
             jax.ShapeDtypeStruct((8, 2 * extent, 2 * extent), jnp.bfloat16),
         ),
-        in_specs=[pl.BlockSpec(memory_space=pltpu.HBM)] * 3,
+        in_specs=[pl.BlockSpec(memory_space=pl.ANY)] * 3,
         out_specs=(vmem,) * 3,
-        scratch_shapes=[
-            pltpu.VMEM(own.shape, jnp.float32),
-            pltpu.VMEM(parts.shape, jnp.float32),
-            pltpu.SemaphoreType.DMA((3,)),
-        ],
+        scratch_shapes=[pltpu.VMEM(parts.shape, jnp.float32), pltpu.SemaphoreType.DMA((3,))],
         compiler_params=pltpu.CompilerParams(vmem_limit_bytes=16 * 1024 * 1024),
         cost_estimate=pl.CostEstimate(flops=0, bytes_accessed=6 * 1024 * 1024, transcendentals=0),
     )(own, patterns, parts)
 
 
-def terms(scalars, planes, upper, near, far, patterns, mats):
+def terms(own_core, scalars, paired, own, other, above_own, above_other, near, far, patterns, odd, mats, start=None):
     extent = patterns.shape[1]
-    rows = planes.shape[1] + extent
+    rows = own.shape[0] // 8 + extent
     smem = pl.BlockSpec(memory_space=pltpu.SMEM)
     vmem = pl.BlockSpec(memory_space=pltpu.VMEM)
+    operands = [scalars, paired, own, other, above_own, above_other, near, far, patterns, odd, mats]
+    if start is None:
+        def body(*refs):
+            return kernel(own_core, *refs[:len(operands)], None, *refs[len(operands):])
+    else:
+        operands.append(start)
+        body = functools.partial(kernel, own_core)
     return pl.pallas_call(
-        kernel,
+        body,
         out_shape=(
-            jax.ShapeDtypeStruct((planes.shape[1] * 8, extent), jnp.float32),
-            jax.ShapeDtypeStruct(upper.shape, jnp.float32),
+            jax.ShapeDtypeStruct(own.shape, jnp.float32),
+            jax.ShapeDtypeStruct(own.shape, jnp.float32),
             jax.ShapeDtypeStruct((2 * MODES, extent, extent), jnp.float32),
         ),
-        in_specs=[smem] + [vmem] * 6,
+        in_specs=[smem] * 2 + [vmem] * (len(operands) - 2),
         out_specs=(vmem,) * 3,
         scratch_shapes=[
             pltpu.VMEM((8, rows, extent), jnp.float32),
             pltpu.VMEM((8, rows, extent), jnp.float32),
             pltpu.VMEM((2 * MODES, extent, extent), jnp.float32),
         ],
-        compiler_params=pltpu.CompilerParams(vmem_limit_bytes=40 * 1024 * 1024),
-    )(scalars, planes, upper, near, far, patterns, mats)
+        compiler_params=pltpu.CompilerParams(vmem_limit_bytes=32 * 1024 * 1024),
+        cost_estimate=pl.CostEstimate(flops=8 * 10**9, bytes_accessed=4 * 1024 * 1024, transcendentals=0),
+    )(*operands)
 
 
 def placed(probe_grad, shape):
@@ -302,30 +328,39 @@
     own = flat(object_slices)
     scalars = jnp.concatenate([row_offsets, col_offsets, counts])
 
-    upper = lax.ppermute(own, "tile", [((i + 1) % size, i) for i in range(size)])
     near = flat(probe_field)
     for bits in (8, 4):
         near = jnp.concatenate([near, partner(near, bits)], axis=0)
-    near, patterns, own = lax.optimization_barrier((near, patterns, own))
     near = jnp.concatenate([near, partner(near, 2)], axis=0)
-    planes, patterns, mats = prepared(own, patterns)
-    near, planes, patterns, mats, scalars = lax.optimization_barrier((near, planes, patterns, mats, scalars))
+    other = partner(own, 1)
+    paired = partner(scalars, 1)
+    odd = partner(patterns.reshape((-1, 2) + patterns.shape[1:])[:, 1], 1)
+    near, late = lax.optimization_barrier((near, own))
+    above = lax.ppermute(late, "tile", [(i, (i - 2) % size if i % 2 == 0 else i) for i in range(size)])
+    own, patterns, mats = prepared(own, patterns)
     far = partner(near, 1)
 
-    own_grad, back, probe_grad = terms(scalars, planes, upper, near, far, patterns, mats)
-
-    back = lax.ppermute(back, "tile", [(i, (i + 1) % size) for i in range(size)])
-    keep, send = placed(probe_grad, near.shape)
-    total = keep + partner(send, 1)
+    keep, send, probe_grad = terms(
+        0, scalars, paired, own, other, other, own, near, far, patterns, odd, mats)
+    got = partner(send, 1)
+    above, probe_grad = lax.optimization_barrier((above, probe_grad))
+    passed, got = lax.optimization_barrier((partner(above, 1), got))
+    keep_late, send_late, probe_grad = terms(
+        1, scalars, paired, own, other, passed, above, near, far, patterns, odd, mats, probe_grad)
+
+    carried = keep_late + partner(send_late, 1)
+    object_grad = keep + got
+    carried = lax.ppermute(carried, "tile", [(i, (i + 2) % size if i % 2 == 0 else i) for i in range(size)])
+    grad_keep, grad_send = placed(probe_grad, near.shape)
+    total = grad_keep + partner(grad_send, 1)
     for bits in (4, 8):
-        keep, send = halved(total)
-        total = keep + partner(send, bits)
-    back, total = lax.optimization_barrier((back, total))
-    keep, send = halved(total)
-    send = partner(send, 2)
-    object_grad = own_grad + back
-    object_grad, send = lax.optimization_barrier((object_grad, send))
-    return unflat(object_grad, object_slices.shape), unflat(keep + send, probe_field.shape)
+        grad_keep, grad_send = halved(total)
+        total = grad_keep + partner(grad_send, bits)
+    grad_keep, grad_send = halved(total)
+    grad_send = partner(grad_send, 2)
+    object_grad = object_grad + carried
+    object_grad, grad_send = lax.optimization_barrier((object_grad, grad_send))
+    return unflat(object_grad, object_slices.shape), unflat(grad_keep + grad_send, probe_field.shape)
 
 
 def solution(mesh):

time: 58.1 us -> 62.2 us (1.071)
  the two profiles are of different devices: /device:TPU:0 before, /device:TPU:4 now
where the time goes in v6:
time: 62.2 us; the launch traced here: 62.4 us
  starting transfers between devices  33.5 us (54%)
  waiting for transfers between devices  15.9 us (26%)
  Pallas kernels  7.99 us (13%)
  other arithmetic  2.39 us (4%)
  between operations  1.51 us (2%)
  local copies, waits for them, and re-layouts  1.13 us (2%)
    ppermute x14, starting transfers between devices, partner(): lax.ppermute(value, 'tile', [(i, i ^ bits) for i in range(lax.axis_size('...  18.7 us
    ppermute x14, waiting for transfers between devices, partner(): lax.ppermute(value, 'tile', [(i, i ^ bits) for i in range(lax.axis_size('...  14.5 us
    ppermute x1, starting transfers between devices, shards(): lax.ppermute(carried, 'tile', [(i, (i + 2) % size if i % 2 == 0 else i) f...  8.35 us
    pallas_call x2, Pallas kernels, terms(): pl.pallas_call(body, out_shape=(jax.ShapeDtypeStruct(own.shape, jnp.float...  6.86 us
    ppermute x1, starting transfers between devices, shards(): lax.ppermute(late, 'tile', [(i, (i - 2) % size if i % 2 == 0 else i) for...  6.45 us
    ppermute x1, waiting for transfers between devices, shards(): lax.ppermute(late, 'tile', [(i, (i - 2) % size if i % 2 == 0 else i) for...  1.35 us
  transfers between devices with their start and end apart: 16, of which 9 were waited for; matrix products, arithmetic and copies ran while one was open for 5% of the time, Pallas kernels for 11%

profile of v6, /device:TPU:4, one launch (start us, length us, event | category | flops | bytes accessed | tf_op | source)
XLA Modules:
  0.0 62.4 jit_solution(15031351192844514814)
XLA Ops:
  0.6 0.0 copy-start
  0.6 2.7 %collective-permute-start.2 = (f32[32,128]{1,0:T(8,128)}, f32[32,128]{1,0:T(8,128)S(1)}, u32[]{:S(2)}, u32[]{:S(2)}) collective-permute-start(f32[32,128]{1,0:T(8,128)} %bitcast.19), channel_id=1, source_target_pairs={{0,8},{1,9},{2,10},{3,11},{4,12},{5,13},{6,14},{7,15},{8,0},{9,1},... | collective-permute-start | bytes 49160 | tf_op jit(solution)/shard_map/ppermute | solution.py:319
  3.3 1.1 %slice_bitcast_fusion = f32[8,128,128]{2,1,0:T(8,128)S(1)} fusion(f32[8,2,128,128]{3,2,1,0:T(8,128)} %bitcast.17), kind=kLoop, calls=%fused_computation | loop fusion | bytes 1048576 | tf_op jit(solution)/shard_map/squeeze | solution.py:337
  4.4 0.0 copy-start.1
  4.4 0.1 collective-permute-start.6
  4.5 0.5 collective-permute-start.1
  5.0 0.6 %collective-permute-done.2 = f32[32,128]{1,0:T(8,128)S(1)} collective-permute-done((f32[32,128]{1,0:T(8,128)}, f32[32,128]{1,0:T(8,128)S(1)}, u32[]{:S(2)}, u32[]{:S(2)}) %collective-permute-start.2) | collective-permute-done | bytes 16416 | tf_op jit(solution)/shard_map/ppermute | solution.py:319
  5.6 0.7 %pad_maximum_fusion.2 = f32[64,128]{1,0:T(8,128)S(1)} fusion(f32[32,128]{1,0:T(8,128)S(1)} %collective-permute-done.2, f32[32,128]{1,0:T(8,128)} %bitcast.20), kind=kLoop, calls=%fused_computation.6 | loop fusion | flops 8192 | bytes 65536 | tf_op jit(solution)/shard_map/concatenate | solution.py:333
  6.3 1.5 %collective-permute-start.3 = (f32[64,128]{1,0:T(8,128)S(1)}, f32[64,128]{1,0:T(8,128)S(1)}, u32[]{:S(2)}, u32[]{:S(2)}) collective-permute-start(f32[64,128]{1,0:T(8,128)S(1)} %pad_maximum_fusion.2), channel_id=1, source_target_pairs={{0,4},{1,5},{2,6},{3,7},{4,0},{5,1},{6,2},{7,3},{8,12},{9,13},{10,... | collective-permute-start | bytes 98312 | tf_op jit(solution)/shard_map/ppermute | solution.py:319
  7.9 2.4 %collective-permute-done.3 = f32[64,128]{1,0:T(8,128)S(1)} collective-permute-done((f32[64,128]{1,0:T(8,128)S(1)}, f32[64,128]{1,0:T(8,128)S(1)}, u32[]{:S(2)}, u32[]{:S(2)}) %collective-permute-start.3) | collective-permute-done | bytes 32800 | tf_op jit(solution)/shard_map/ppermute | solution.py:319
  10.2 0.0 copy-done.2
  10.3 1.6 %collective-permute-start.4 = (f32[128,128]{1,0:T(8,128)S(1)}, f32[128,128]{1,0:T(8,128)S(1)}, u32[]{:S(2)}, u32[]{:S(2)}) collective-permute-start(f32[128,128]{1,0:T(8,128)S(1)} %pad_maximum_fusion.1), channel_id=1, source_target_pairs={{0,2},{1,3},{2,0},{3,1},{4,6},{5,7},{6,4},{7,5},{8,10},{9,11},{10,... | collective-permute-start | bytes 196616 | tf_op jit(solution)/shard_map/ppermute | solution.py:319
  11.8 2.8 %collective-permute-done.4 = f32[128,128]{1,0:T(8,128)S(1)} collective-permute-done((f32[128,128]{1,0:T(8,128)S(1)}, f32[128,128]{1,0:T(8,128)S(1)}, u32[]{:S(2)}, u32[]{:S(2)}) %collective-permute-start.4) | collective-permute-done | bytes 65568 | tf_op jit(solution)/shard_map/ppermute | solution.py:319
  14.6 0.0 copy-start.3
  14.6 0.0 copy-start.4
  14.6 0.1 collective-permute-start.5
  15.3 0.0 copy-done.3
  15.4 0.1 pad_add_fusion.refs_0_.scalars_ref
  15.4 0.5 collective-permute-start
  16.0 0.0 copy-done.1
  16.0 1.1 %shard_map.86 = (f32[1024,128]{1,0:T(8,128)S(1)}, f32[16,128,128]{2,1,0:T(8,128)S(1)}, bf16[8,256,256]{2,1,0:T(8,128)(2,1)S(1)}) custom-call(f32[1024,128]{1,0:T(8,128)} %bitcast.2.own_ref, f32[16,128,128]{2,1,0:T(8,128)S(1)} %copy-done, f32[4,128,128]{2,1,0:T(8,128)S(1)} %copy-done.1), custom_call_target="tpu_custom_call" | custom-call | bytes 6291456 | tf_op jit(solution)/shard_map/pallas_call | solution.py:250
  17.1 6.4 %collective-permute-start.7 = (f32[1024,128]{1,0:T(8,128)}, f32[1024,128]{1,0:T(8,128)S(1)}, u32[]{:S(2)}, u32[]{:S(2)}) collective-permute-start(f32[1024,128]{1,0:T(8,128)} %bitcast.2.own_ref), channel_id=1, source_target_pairs={{0,14},{1,1},{2,0},{3,3},{4,2},{5,5},{6,4},{7,7},{8,6},{9,9},{10,8... | collective-permute-start | bytes 1572872 | tf_op jit(solution)/shard_map/ppermute | solution.py:339
  23.5 0.0 collective-permute-done.refs_1_.paired_ref
  23.5 0.0 collective-permute-done.5.refs_7_.far_ref
  23.5 0.0 collective-permute-done.6.refs_9_.odd_ref
  23.5 0.0 collective-permute-done.1.refs_3_.refs_4_.other_ref
  23.6 5.5 %shard_map.87 = (f32[1024,128]{1,0:T(8,128)S(1)}, f32[1024,128]{1,0:T(8,128)S(1)}, f32[4,128,128]{2,1,0:T(8,128)S(1)}) custom-call(s32[33]{0:T(128)S(1)} %pad_add_fusion.refs_0_.scalars_ref, s32[33]{0:T(128)S(1)} %collective-permute-done.refs_1_.paired_ref, f32[1024,128]{1,0:T(8,128)S(1)} %get-tuple-element.21.refs_2_.refs_5_.own_ref, ...), custom_call_target="tpu_custom_call" | custom-call | flops 8000000000 | bytes 4194304 | tf_op jit(solution)/shard_map/pallas_call | solution.py:277
  29.1 0.1 collective-permute-start.9
  29.2 1.3 %collective-permute-done.7.above_other_ref = f32[1024,128]{1,0:T(8,128)S(1)} collective-permute-done((f32[1024,128]{1,0:T(8,128)}, f32[1024,128]{1,0:T(8,128)S(1)}, u32[]{:S(2)}, u32[]{:S(2)}) %collective-permute-start.7) | collective-permute-done | bytes 524320 | tf_op jit(solution)/shard_map/ppermute | solution.py:339
  30.5 0.0 collective-permute-start.8
  30.5 0.5 collective-permute-done.9
  31.1 1.4 %collective-permute-done.8.above_own_ref = f32[1024,128]{1,0:T(8,128)S(1)} collective-permute-done((f32[1024,128]{1,0:T(8,128)S(1)}, f32[1024,128]{1,0:T(8,128)S(1)}, u32[]{:S(2)}, u32[]{:S(2)}) %collective-permute-start.8) | collective-permute-done | bytes 524320 | tf_op jit(solution)/shard_map/ppermute | solution.py:319
  32.4 1.3 %shard_map.88 = (f32[1024,128]{1,0:T(8,128)S(1)}, f32[1024,128]{1,0:T(8,128)S(1)}, f32[4,128,128]{2,1,0:T(8,128)S(1)}) custom-call(s32[33]{0:T(128)S(1)} %pad_add_fusion.refs_0_.scalars_ref, s32[33]{0:T(128)S(1)} %collective-permute-done.refs_1_.paired_ref, f32[1024,128]{1,0:T(8,128)S(1)} %get-tuple-element.21.refs_2_.refs_5_.own_ref, ...), custom_call_target="tpu_custom_call" | custom-call | flops 8000000000 | bytes 4194304 | tf_op jit(solution)/shard_map/pallas_call | solution.py:277
  33.8 3.0 %collective-permute-start.10 = (f32[1024,128]{1,0:T(8,128)S(1)}, f32[1024,128]{1,0:T(8,128)S(1)}, u32[]{:S(2)}, u32[]{:S(2)}) collective-permute-start(f32[1024,128]{1,0:T(8,128)S(1)} %get-tuple-element.34), channel_id=1, source_target_pairs={{0,1},{1,0},{2,3},{3,2},{4,5},{5,4},{6,7},{7,6},{8,9},{9,8},{10,11... | collective-permute-start | bytes 1572872 | tf_op jit(solution)/shard_map/ppermute | solution.py:319
  36.8 0.1 collective-permute-start.12
  36.9 1.6 %collective-permute-done.12 = f32[256,128]{1,0:T(8,128)S(1)} collective-permute-done((f32[256,128]{1,0:T(8,128)S(1)}, f32[256,128]{1,0:T(8,128)S(1)}, u32[]{:S(2)}, u32[]{:S(2)}) %collective-permute-start.12) | collective-permute-done | bytes 131104 | tf_op jit(solution)/shard_map/ppermute | solution.py:319
  38.5 0.1 collective-permute-start.13
  38.6 0.0 collective-permute-done.10
  38.6 0.1 add.22
  38.7 8.4 %collective-permute-start.11 = (f32[1024,128]{1,0:T(8,128)S(1)}, f32[1024,128]{1,0:T(8,128)S(1)}, u32[]{:S(2)}, u32[]{:S(2)}) collective-permute-start(f32[1024,128]{1,0:T(8,128)S(1)} %add.22), channel_id=1, source_target_pairs={{0,2},{1,1},{2,4},{3,3},{4,6},{5,5},{6,8},{7,7},{8,10},{9,9},{10,1... | collective-permute-start | bytes 1572872 | tf_op jit(solution)/shard_map/ppermute | solution.py:353
  47.0 0.0 collective-permute-done.13
  47.1 0.5 collective-permute-start.14
  47.6 4.4 %collective-permute-done.14 = f32[64,128]{1,0:T(8,128)S(1)} collective-permute-done((f32[64,128]{1,0:T(8,128)S(1)}, f32[64,128]{1,0:T(8,128)S(1)}, u32[]{:S(2)}, u32[]{:S(2)}) %collective-permute-start.14) | collective-permute-done | bytes 32800 | tf_op jit(solution)/shard_map/ppermute | solution.py:319
  51.9 8.1 %collective-permute-start.15 = (f32[32,128]{1,0:T(8,128)S(1)}, f32[32,128]{1,0:T(8,128)S(1)}, u32[]{:S(2)}, u32[]{:S(2)}) collective-permute-start(f32[32,128]{1,0:T(8,128)S(1)} %slice.33), channel_id=1, source_target_pairs={{0,2},{1,3},{2,0},{3,1},{4,6},{5,7},{6,4},{7,5},{8,10},{9,11},{10,... | collective-permute-start | bytes 49160 | tf_op jit(solution)/shard_map/ppermute | solution.py:319
  60.1 0.0 collective-permute-done.11
  60.1 0.9 %add_add_fusion = f32[1024,128]{1,0:T(8,128)} fusion(f32[1024,128]{1,0:T(8,128)S(1)} %collective-permute-done.11, f32[1024,128]{1,0:T(8,128)S(1)} %get-tuple-element.25, f32[1024,128]{1,0:T(8,128)S(1)} %collective-permute-done.9), kind=kLoop, calls=%fused_computation.1 | loop fusion | flops 262144 | bytes 2097152 | tf_op jit(solution)/shard_map/add | solution.py:361
  61.0 0.8 %collective-permute-done.15 = f32[32,128]{1,0:T(8,128)S(1)} collective-permute-done((f32[32,128]{1,0:T(8,128)S(1)}, f32[32,128]{1,0:T(8,128)S(1)}, u32[]{:S(2)}, u32[]{:S(2)}) %collective-permute-start.15) | collective-permute-done | bytes 16416 | tf_op jit(solution)/shard_map/ppermute | solution.py:319
  61.8 0.6 slice_add_fusion.2
  (12 shorter events, 0.1 us)
Async XLA Ops:
  0.6 15.3 %copy-start = (f32[16,128,128]{2,1,0:T(8,128)S(1)}, f32[16,128,128]{2,1,0:T(8,128)}, u32[]{:S(2)}) copy-start(f32[16,128,128]{2,1,0:T(8,128)} %patterns_ref.1) | copy-start | bytes 3145732
  0.6 5.0 %collective-permute-start.2 = (f32[32,128]{1,0:T(8,128)}, f32[32,128]{1,0:T(8,128)S(1)}, u32[]{:S(2)}, u32[]{:S(2)}) collective-permute-start(f32[32,128]{1,0:T(8,128)} %bitcast.19), channel_id=1, source_target_pairs={{0,8},{1,9},{2,10},{3,11},{4,12},{5,13},{6,14},{7,15},{8,0},{9,1},... | collective-permute-start | bytes 49160 | tf_op jit(solution)/shard_map/ppermute | solution.py:319
  3.3 7.0 %copy-start.2 = (f32[8,2,2,128]{3,2,1,0:T(2,128)S(1)}, f32[8,2,2,128]{3,2,1,0:T(2,128)}, u32[]{:S(2)}) copy-start(f32[8,2,2,128]{3,2,1,0:T(2,128)} %param.8) | copy-start | bytes 49156
  4.4 11.6 %copy-start.1 = (f32[4,128,128]{2,1,0:T(8,128)S(1)}, f32[4,128,128]{2,1,0:T(8,128)}, u32[]{:S(2)}) copy-start(f32[4,128,128]{2,1,0:T(8,128)} %constant.2.clone.factors_ref) | copy-start | bytes 786436
  4.4 19.1 %collective-permute-start.6 = (f32[8,128,128]{2,1,0:T(8,128)S(1)}, f32[8,128,128]{2,1,0:T(8,128)S(1)}, u32[]{:S(2)}, u32[]{:S(2)}) collective-permute-start(f32[8,128,128]{2,1,0:T(8,128)S(1)} %slice_bitcast_fusion), channel_id=1, source_target_pairs={{0,1},{1,0},{2,3},{3,2},{4,5},{5,4},{6,7},{7,6},{8,9},{9,8},{10,11... | collective-permute-start | bytes 1572872 | tf_op jit(solution)/shard_map/ppermute | solution.py:319
  4.5 19.1 %collective-permute-start.1 = (f32[1024,128]{1,0:T(8,128)}, f32[1024,128]{1,0:T(8,128)S(1)}, u32[]{:S(2)}, u32[]{:S(2)}) collective-permute-start(f32[1024,128]{1,0:T(8,128)} %bitcast.2.own_ref), channel_id=1, source_target_pairs={{0,1},{1,0},{2,3},{3,2},{4,5},{5,4},{6,7},{7,6},{8,9},{9,8},{10,11... | collective-permute-start | bytes 1572872 | tf_op jit(solution)/shard_map/ppermute | solution.py:319
  6.3 3.9 %collective-permute-start.3 = (f32[64,128]{1,0:T(8,128)S(1)}, f32[64,128]{1,0:T(8,128)S(1)}, u32[]{:S(2)}, u32[]{:S(2)}) collective-permute-start(f32[64,128]{1,0:T(8,128)S(1)} %pad_maximum_fusion.2), channel_id=1, source_target_pairs={{0,4},{1,5},{2,6},{3,7},{4,0},{5,1},{6,2},{7,3},{8,12},{9,13},{10,... | collective-permute-start | bytes 98312 | tf_op jit(solution)/shard_map/ppermute | solution.py:319
  10.3 4.3 %collective-permute-start.4 = (f32[128,128]{1,0:T(8,128)S(1)}, f32[128,128]{1,0:T(8,128)S(1)}, u32[]{:S(2)}, u32[]{:S(2)}) collective-permute-start(f32[128,128]{1,0:T(8,128)S(1)} %pad_maximum_fusion.1), channel_id=1, source_target_pairs={{0,2},{1,3},{2,0},{3,1},{4,6},{5,7},{6,4},{7,5},{8,10},{9,11},{10,... | collective-permute-start | bytes 196616 | tf_op jit(solution)/shard_map/ppermute | solution.py:319
  14.6 0.8 %copy-start.3 = (s32[16]{0:T(128)S(1)}, s32[16]{0:T(128)}, u32[]{:S(2)}) copy-start(s32[16]{0:T(128)} %param.11) | copy-start | bytes 196
  14.6 0.8 %copy-start.4 = (s32[16]{0:T(128)S(1)}, s32[16]{0:T(128)}, u32[]{:S(2)}) copy-start(s32[16]{0:T(128)} %param.10) | copy-start | bytes 196
  14.6 8.9 %collective-permute-start.5 = (f32[256,128]{1,0:T(8,128)S(1)}, f32[256,128]{1,0:T(8,128)S(1)}, u32[]{:S(2)}, u32[]{:S(2)}) collective-permute-start(f32[256,128]{1,0:T(8,128)S(1)} %pad_maximum_fusion.refs_6_.near_ref), channel_id=1, source_target_pairs={{0,1},{1,0},{2,3},{3,2},{4,5},{5,4},{6,7},{7,6},{8,9},{9,8},{10,11... | collective-permute-start | bytes 393224 | tf_op jit(solution)/shard_map/ppermute | solution.py:319
  15.4 8.1 %collective-permute-start = (s32[33]{0:T(128)S(1)}, s32[33]{0:T(128)S(1)}, u32[]{:S(2)}, u32[]{:S(2)}) collective-permute-start(s32[33]{0:T(128)S(1)} %pad_add_fusion.refs_0_.scalars_ref), channel_id=1, source_target_pairs={{0,1},{1,0},{2,3},{3,2},{4,5},{5,4},{6,7},{7,6},{8,9},{9,8},{10,11... | collective-permute-start | bytes 404 | tf_op jit(solution)/shard_map/ppermute | solution.py:319
  17.1 13.4 %collective-permute-start.7 = (f32[1024,128]{1,0:T(8,128)}, f32[1024,128]{1,0:T(8,128)S(1)}, u32[]{:S(2)}, u32[]{:S(2)}) collective-permute-start(f32[1024,128]{1,0:T(8,128)} %bitcast.2.own_ref), channel_id=1, source_target_pairs={{0,14},{1,1},{2,0},{3,3},{4,2},{5,5},{6,4},{7,7},{8,6},{9,9},{10,8... | collective-permute-start | bytes 1572872 | tf_op jit(solution)/shard_map/ppermute | solution.py:339
  29.1 2.0 %collective-permute-start.9 = (f32[1024,128]{1,0:T(8,128)S(1)}, f32[1024,128]{1,0:T(8,128)S(1)}, u32[]{:S(2)}, u32[]{:S(2)}) collective-permute-start(f32[1024,128]{1,0:T(8,128)S(1)} %get-tuple-element.29), channel_id=1, source_target_pairs={{0,1},{1,0},{2,3},{3,2},{4,5},{5,4},{6,7},{7,6},{8,9},{9,8},{10,11... | collective-permute-start | bytes 1572872 | tf_op jit(solution)/shard_map/ppermute | solution.py:319
  30.5 1.9 %collective-permute-start.8 = (f32[1024,128]{1,0:T(8,128)S(1)}, f32[1024,128]{1,0:T(8,128)S(1)}, u32[]{:S(2)}, u32[]{:S(2)}) collective-permute-start(f32[1024,128]{1,0:T(8,128)S(1)} %collective-permute-done.7.above_other_ref), channel_id=1, source_target_pairs={{0,1},{1,0},{2,3},{3,2},{4,5},{5,4},{6,7},{7,6},{8,9},{9,8},{10,11... | collective-permute-start | bytes 1572872 | tf_op jit(solution)/shard_map/ppermute | solution.py:319
  33.8 4.8 %collective-permute-start.10 = (f32[1024,128]{1,0:T(8,128)S(1)}, f32[1024,128]{1,0:T(8,128)S(1)}, u32[]{:S(2)}, u32[]{:S(2)}) collective-permute-start(f32[1024,128]{1,0:T(8,128)S(1)} %get-tuple-element.34), channel_id=1, source_target_pairs={{0,1},{1,0},{2,3},{3,2},{4,5},{5,4},{6,7},{7,6},{8,9},{9,8},{10,11... | collective-permute-start | bytes 1572872 | tf_op jit(solution)/shard_map/ppermute | solution.py:319
  36.8 1.7 %collective-permute-start.12 = (f32[256,128]{1,0:T(8,128)S(1)}, f32[256,128]{1,0:T(8,128)S(1)}, u32[]{:S(2)}, u32[]{:S(2)}) collective-permute-start(f32[256,128]{1,0:T(8,128)S(1)} %get-tuple-element.37), channel_id=1, source_target_pairs={{0,1},{1,0},{2,3},{3,2},{4,5},{5,4},{6,7},{7,6},{8,9},{9,8},{10,11... | collective-permute-start | bytes 393224 | tf_op jit(solution)/shard_map/ppermute | solution.py:319
  38.5 8.5 %collective-permute-start.13 = (f32[128,128]{1,0:T(8,128)S(1)}, f32[128,128]{1,0:T(8,128)S(1)}, u32[]{:S(2)}, u32[]{:S(2)}) collective-permute-start(f32[128,128]{1,0:T(8,128)S(1)} %slice.30), channel_id=1, source_target_pairs={{0,4},{1,5},{2,6},{3,7},{4,0},{5,1},{6,2},{7,3},{8,12},{9,13},{10,... | collective-permute-start | bytes 196616 | tf_op jit(solution)/shard_map/ppermute | solution.py:319
  38.7 21.4 %collective-permute-start.11 = (f32[1024,128]{1,0:T(8,128)S(1)}, f32[1024,128]{1,0:T(8,128)S(1)}, u32[]{:S(2)}, u32[]{:S(2)}) collective-permute-start(f32[1024,128]{1,0:T(8,128)S(1)} %add.22), channel_id=1, source_target_pairs={{0,2},{1,1},{2,4},{3,3},{4,6},{5,5},{6,8},{7,7},{8,10},{9,9},{10,1... | collective-permute-start | bytes 1572872 | tf_op jit(solution)/shard_map/ppermute | solution.py:353
  47.1 4.9 %collective-permute-start.14 = (f32[64,128]{1,0:T(8,128)S(1)}, f32[64,128]{1,0:T(8,128)S(1)}, u32[]{:S(2)}, u32[]{:S(2)}) collective-permute-start(f32[64,128]{1,0:T(8,128)S(1)} %slice.32), channel_id=1, source_target_pairs={{0,8},{1,9},{2,10},{3,11},{4,12},{5,13},{6,14},{7,15},{8,0},{9,1},... | collective-permute-start | bytes 98312 | tf_op jit(solution)/shard_map/ppermute | solution.py:319
  51.9 9.9 %collective-permute-start.15 = (f32[32,128]{1,0:T(8,128)S(1)}, f32[32,128]{1,0:T(8,128)S(1)}, u32[]{:S(2)}, u32[]{:S(2)}) collective-permute-start(f32[32,128]{1,0:T(8,128)S(1)} %slice.33), channel_id=1, source_target_pairs={{0,2},{1,3},{2,0},{3,1},{4,6},{5,7},{6,4},{7,5},{8,10},{9,11},{10,... | collective-permute-start | bytes 49160 | tf_op jit(solution)/shard_map/ppermute | solution.py:319
